TPU v7x, 512 devices: a whole 4x4x16 slice. The times are simulated.
512 devices in a mesh: ctx: 16 (over y, x), exp: 32 (over z, core).
Axes of the slice: x: 4, y: 4, z: 16, core: 2. Of those that a mesh axis runs over, the one named last changes fastest.
Arguments:
- mixed_qkv: bfloat16 [32, 2048, 3072], P('exp', 'ctx'), may hold values from -6 to 6
- conv_weight: bfloat16 [4, 3072], replicated, may hold values from -2.5 to 2.5
- log_gate: float32 [32, 2048, 8], P('exp', 'ctx'), may hold values from -1 to 0
- beta: float32 [32, 2048, 8], P('exp', 'ctx'), may hold values from 0.005 to 0.05
- gate_z: bfloat16 [32, 2048, 1024], P('exp', 'ctx'), may hold values from -6 to 6
- norm_gain: float32 [128], replicated, may hold values from 0.1 to 1.9
- out_weight: bfloat16 [1024, 2048], P('exp', 'ctx'), may hold values from -0.1875 to 0.1875
- residual: bfloat16 [32, 2048, 2048], P('exp', 'ctx'), may hold values from -6 to 6
- post_gain: float32 [2048], replicated, may hold values from 0.1 to 1.9
- expert_ids: int32 [32, 2048, 1], P('exp', 'ctx'), may hold values from 0 to 31; in each aligned block of 128 rows (0 to 127, 128 to 255, ..., all dimensions but the last counted through in order) at most 8 rows name the same one
- route_weight: float32 [32, 2048, 1], P('exp', 'ctx'), may hold values from 0.2 to 1
- w_gate: bfloat16 [32, 2048, 512], P('exp', 'ctx'), may hold values from -0.125 to 0.125
- w_up: bfloat16 [32, 2048, 512], P('exp', 'ctx'), may hold values from -0.125 to 0.125
- w_down: bfloat16 [32, 512, 2048], P('exp', None, 'ctx'), may hold values from -0.25 to 0.25
Outputs:
- mixed: bfloat16 [32, 2048, 2048], P('exp', 'ctx')
Inputs may be any that keep to these rules, and one draw needn't show every extreme that they name: `expert_ids`: among the rows of one device, at most 8 picks name the same expert, a bound that some block reaches.
All inputs are finite; a program needn't handle non-finite values.
Results may differ from a plain program's by a relative error of at most 0.0057.
Values may be sent and summed in bfloat16 or wider, within the bound.
A program may use at most 128 MiB of HBM per device.

v0:
```python
import jax
import jax.numpy as jnp
from jax import lax
from jax.sharding import PartitionSpec as P

GROUP = 64


exact_mode = lax.Precision.HIGHEST
norm_eps = 1e-06


def shifted(block, axis, distance):
    devices = range(lax.axis_size(axis))
    route = [(i - distance, i) for i in devices if i - distance in devices]
    return lax.ppermute(block, axis, route)


def carried_in(array, axis, combine, identity):
    count, here = (lax.axis_size(axis), lax.axis_index(axis))
    everything = jax.tree.map(lambda part: lax.all_gather(part, axis), array)
    start = jax.tree.map(
        lambda part, zero: jnp.broadcast_to(jnp.asarray(zero, part.dtype), part.shape),
        array,
        identity,
    )

    def turn(k, before):
        reached = k < here
        new = combine(before, jax.tree.map(lambda part: part[k], everything))
        return jax.tree.map(lambda a, b: jnp.where(reached, a, b), new, before)

    return lax.fori_loop(0, count, turn, start)


def unit_rows(rows):
    return rows * lax.rsqrt(jnp.sum(rows * rows, axis=-1, keepdims=True) + norm_eps)


def to_blocks(array, blocks, size):
    return jnp.moveaxis(array.reshape((blocks, size) + array.shape[1:]), 2, 0)


def apply_state(block_map, state):
    return jnp.einsum("hcd,hde->hce", block_map, state, precision=exact_mode)


def compose(block_transit, state):
    return jnp.einsum("hde,hef->hdf", block_transit, state, precision=exact_mode)


def on_device(
    mixed_qkv,
    conv_weight,
    log_gate,
    beta,
    gate_z,
    norm_gain,
    out_weight,
    residual,
    post_gain,
    expert_ids,
    route_weight,
    w_gate,
    w_up,
    w_down,
):
    inputs = mixed_qkv[0]
    tokens_here, width = inputs.shape
    taps = conv_weight.shape[0]
    tail = shifted(inputs[tokens_here - (taps - 1) :], "ctx", 1)
    padded = jnp.concatenate([tail, inputs], axis=0).astype(jnp.float32)
    filters = conv_weight.astype(jnp.float32)
    filtered = padded[0:tokens_here] * filters[0]
    for offset in range(1, taps):
        filtered = filtered + padded[offset : offset + tokens_here] * filters[offset]
    active = jax.nn.silu(filtered)
    heads = log_gate.shape[2]
    head_dim = width // (3 * heads)
    inner = heads * head_dim
    queries = unit_rows(active[:, :inner].reshape(tokens_here, heads, head_dim)) * head_dim ** (
        -0.5
    )
    keys = unit_rows(active[:, inner : 2 * inner].reshape(tokens_here, heads, head_dim))
    values = active[:, 2 * inner :].reshape(tokens_here, heads, head_dim)
    blocks = tokens_here // GROUP
    query_blocks = to_blocks(queries, blocks, GROUP)
    key_blocks = to_blocks(keys, blocks, GROUP)
    value_blocks = to_blocks(values, blocks, GROUP)
    decay_sum = jnp.cumsum(to_blocks(log_gate[0], blocks, GROUP), axis=-1)
    strength = to_blocks(beta[0], blocks, GROUP)
    position = jnp.arange(GROUP)
    causal = position[:, None] >= position[None, :]
    strict = position[:, None] > position[None, :]
    spread = decay_sum[..., :, None] - decay_sum[..., None, :]
    decay_pair = jnp.where(causal, jnp.exp(jnp.where(causal, spread, 0.0)), 0.0)
    key_key = jnp.einsum("hncd,hnsd->hncs", key_blocks, key_blocks, precision=exact_mode)
    lower = jnp.where(strict, strength[..., :, None] * decay_pair * key_key, 0.0)
    system = lower + jnp.eye(GROUP, dtype=jnp.float32)
    growth = jnp.exp(decay_sum)
    right = jnp.concatenate(
        [strength[..., None] * value_blocks, (strength * growth)[..., None] * key_blocks], axis=-1
    )
    solved = jax.scipy.linalg.solve_triangular(system, right, lower=True, unit_diagonal=True)
    written = solved[..., :head_dim]
    erased = solved[..., head_dim:]
    query_key = decay_pair * jnp.einsum(
        "hncd,hnsd->hncs", query_blocks, key_blocks, precision=exact_mode
    )
    query_map = growth[..., None] * query_blocks - jnp.einsum(
        "hncs,hnsd->hncd", query_key, erased, precision=exact_mode
    )
    local_out = jnp.einsum("hncs,hnsd->hncd", query_key, written, precision=exact_mode)
    carried = jnp.exp(decay_sum[..., -1:] - decay_sum)[..., None] * key_blocks
    identity_mat = jnp.eye(head_dim, dtype=jnp.float32)
    transit = jnp.exp(decay_sum[..., -1])[..., None, None] * identity_mat - jnp.einsum(
        "hncd,hnce->hnde", carried, erased, precision=exact_mode
    )
    deposit = jnp.einsum("hncd,hnce->hnde", carried, written, precision=exact_mode)
    per_block = tuple(
        (jnp.moveaxis(member, 1, 0) for member in (query_map, local_out, transit, deposit))
    )

    def first_pass(carry, member):
        map_state, value_state = carry
        block_map, block_out, block_transit, block_deposit = member
        out_map = apply_state(block_map, map_state)
        out_value = apply_state(block_map, value_state) + block_out
        map_state = compose(block_transit, map_state)
        value_state = compose(block_transit, value_state) + block_deposit
        return ((map_state, value_state), (out_map, out_value))

    identity_stack = jnp.broadcast_to(identity_mat, (heads, head_dim, head_dim))
    zero_stack = jnp.zeros((heads, head_dim, head_dim), jnp.float32)
    (transfer, ending), (outs_map, outs_value) = lax.scan(
        first_pass, (identity_stack, zero_stack), per_block
    )

    def combine(earlier, later):
        return (compose(later[0], earlier[0]), compose(later[0], earlier[1]) + later[1])

    prior = carried_in((transfer, ending), "ctx", combine, (identity_stack, zero_stack))
    incoming = prior[1]

    def second_pass(state, member):
        block_map, block_out, block_transit, block_deposit = member
        result = apply_state(block_map, state) + block_out
        state = compose(block_transit, state) + block_deposit
        return (state, result)

    unused, core_blocks = lax.scan(second_pass, incoming, per_block)
    core = jnp.moveaxis(core_blocks, 1, 2).reshape(tokens_here, heads, head_dim)
    gates = gate_z[0].astype(jnp.float32).reshape(tokens_here, heads, head_dim)
    scale_rms = lax.rsqrt(jnp.mean(core * core, axis=-1, keepdims=True) + norm_eps)
    normed = (
        (core * scale_rms * norm_gain * jax.nn.silu(gates))
        .reshape(tokens_here, inner)
        .astype(jnp.bfloat16)
    )
    model_dim = residual.shape[2]
    band = lax.all_gather(out_weight, "ctx", axis=1, tiled=True)
    attended = jnp.dot(
        normed, lax.all_gather(band, "exp", axis=0, tiled=True), preferred_element_type=jnp.float32
    )
    hidden = (residual[0].astype(jnp.float32) + attended).astype(jnp.bfloat16)
    stream = lax.optimization_barrier(hidden).astype(jnp.float32)
    routed_in = (
        stream * lax.rsqrt(jnp.mean(stream * stream, axis=-1, keepdims=True) + norm_eps) * post_gain
    ).astype(jnp.bfloat16)
    expert_count = lax.axis_size("exp")
    picks = expert_ids.shape[2]
    capacity = 2 * picks * tokens_here // expert_count
    routed = expert_ids[0].reshape(tokens_here * picks)
    member_of = (routed[:, None] == jnp.arange(expert_count, dtype=jnp.int32)[None, :]).astype(
        jnp.int32
    )
    ranks = jnp.cumsum(member_of, axis=0)
    slot_of = jnp.sum(ranks * member_of, axis=1) - 1
    target = routed * capacity + slot_of
    repeated = routed_in[:, None, :].reshape(tokens_here * picks, model_dim)
    outbound = (
        jnp.zeros((expert_count * capacity, model_dim), jnp.bfloat16).at[target].set(repeated)
    )
    outbound = outbound.reshape(expert_count, capacity, model_dim)
    gate_full, up_full, down_full = (
        lax.all_gather(w_gate[0], "ctx", axis=0, tiled=True),
        lax.all_gather(w_up[0], "ctx", axis=0, tiled=True),
        lax.all_gather(w_down[0], "ctx", axis=1, tiled=True),
    )
    arrived = lax.all_to_all(outbound, "exp", split_axis=0, concat_axis=0, tiled=True)
    flat = arrived.reshape(-1, model_dim)
    gate_part = jnp.dot(flat, gate_full, preferred_element_type=jnp.float32)
    up_part = jnp.dot(flat, up_full, preferred_element_type=jnp.float32)
    activated = (jax.nn.silu(gate_part) * up_part).astype(jnp.bfloat16)
    answer = jnp.dot(activated, down_full, preferred_element_type=jnp.float32).astype(jnp.bfloat16)
    returned = lax.all_to_all(
        answer.reshape(arrived.shape), "exp", split_axis=0, concat_axis=0, tiled=True
    )
    fetched = returned.reshape(expert_count * capacity, model_dim)[target].astype(jnp.float32)
    fetched = fetched.reshape(tokens_here, picks, model_dim)
    mixed = stream + jnp.sum(route_weight[0][..., None] * fetched, axis=1)
    return mixed.astype(jnp.bfloat16)[None]


def solution(mesh):
    placed = (
        P("exp", "ctx", None),
        P(),
        P("exp", "ctx", None),
        P("exp", "ctx", None),
        P("exp", "ctx", None),
        P(),
        P("exp", "ctx"),
        P("exp", "ctx", None),
        P(),
        P("exp", "ctx", None),
        P("exp", "ctx", None),
        P("exp", "ctx", None),
        P("exp", "ctx", None),
        P("exp", None, "ctx"),
    )
    return jax.shard_map(
        on_device, mesh=mesh, in_specs=placed, out_specs=P("exp", "ctx", None), check_vma=False
    )
```

profile of v0, /device:TPU:1, one launch (start us, length us, event | category | flops | bytes accessed | tf_op | source)
XLA Modules:
  0.0 634.5 jit_solution(14538000550936790094)
XLA Ops:
  7.4 3.9 collective-permute-start
  14.8 1.3 maximum_convert_fusion
  17.1 1.3 multiply_bitcast_fusion
  20.2 78.6 %custom-call.4 = f32[8,2,1,64,64]{3,4,2,1,0:T(8,128)S(1)} custom-call(f32[8,2,1,64,64]{4,3,2,1,0:T(8,128)S(1)} %fusion.45), custom_call_target="InvertDiagBlocksLowerTriangular" | custom-call | tf_op jit(solution)/shard_map/jit(_solve_triangular)/vmap(vmap())/triangular_solve | solution.py:104
  100.5 2.1 convolution_bitcast_fusion
  102.7 2.2 fusion.37
  105.1 2.9 while.40
  109.6 20.3 %all_gather.31 = bf16[32,2048]{1,0:T(8,128)(2,1)} all-gather(bf16[32,128]{1,0:T(8,128)(2,1)S(1)} %copy-done.8), channel_id=1, replica_groups=mesh['ctx'=16,'exp'=32] {'ctx'}, dimensions={1}, use_global_device_ids=true | all-gather | bytes 139264 | tf_op jit(solution)/shard_map/all_gather | solution.py:161
  131.6 2.0 copy.109
  133.5 1.2 reduce_sum.50
  134.9 1.2 copy.108
  138.0 1.6 fusion.46
  139.6 60.0 %all-gather.14.cloned.1.call-done = f32[128,128,128]{2,1,0:T(8,128)} async-done(((f32[8,128,128]{2,1,0:T(8,128)}), f32[128,128,128]{2,1,0:T(8,128)}) %all-gather.14.cloned.1.call-update) | async-done | bytes 8388624 | tf_op jit(solution)/shard_map/all_gather | solution.py:21
  199.6 88.9 %all-gather.16.cloned.1.call-done = f32[128,128,128]{2,1,0:T(8,128)} async-done(((f32[8,128,128]{2,1,0:T(8,128)}), f32[128,128,128]{2,1,0:T(8,128)}) %all-gather.16.cloned.1.call-update) | async-done | bytes 8388624 | tf_op jit(solution)/shard_map/all_gather | solution.py:21
  288.5 31.5 %while.41 = (s32[]{:T(128)}, f32[8,128,128]{2,1,0:T(8,128)S(1)}, s32[]{:T(128)}, f32[16,8,128,128]{3,2,1,0:T(8,128)}, f32[16,8,128,128]{3,2,1,0:T(8,128)}, /*index=5*/s32[]{:T(128)}, s32[]{:T(128)}) while((s32[]{:T(128)}, f32[8,128,128]{2,1,0:T(8,128)S(1)}, s32[]{:T(128)}, f32[16,8,128,128]{3,2,1,0:T(8,128)}, ...), condition=%wide.region_5.6_spmd.clone, body=%wide.region_4.5_spmd.clone.sunk | while | flops 201850880 | bytes 3672671 | solution.py:33
  288.5 1.9 fusion.145
  290.5 1.9 fusion.145
  292.4 1.9 fusion.145
  294.4 1.9 fusion.145
  296.4 1.9 fusion.145
  298.3 1.9 fusion.145
  300.3 1.9 fusion.145
  302.3 1.9 fusion.145
  304.2 1.9 fusion.145
  306.2 1.9 fusion.145
  308.2 1.9 fusion.145
  310.2 1.9 fusion.145
  312.2 1.9 fusion.145
  314.1 1.9 fusion.145
  316.1 1.9 fusion.145
  318.1 1.9 fusion.145
  320.0 6.0 while.39
  320.1 2.3 fusion.137
  323.1 2.3 fusion.137
  326.0 1.3 multiply_reduce_fusion
  327.5 1.4 copy.97
  328.9 35.7 %all-gather.12.cloned.1.call-done = bf16[1024,2048]{1,0:T(8,128)(2,1)} async-done(((bf16[32,2048]{1,0:T(8,128)(2,1)}), bf16[1024,2048]{1,0:T(8,128)(2,1)}) %all-gather.12.cloned.1.call-update) | async-done | bytes 4194320 | tf_op jit(solution)/shard_map/all_gather | solution.py:163
  364.8 3.1 fusion.28
  368.1 2.5 scatter_custom_fusion
  370.7 8.5 %all-to-all-start = ((bf16[32,8,2048]{2,1,0:T(8,128)(2,1)}), bf16[32,8,2048]{2,1,0:T(8,128)(2,1)S(1)}, u32[]{:S(2)}, u32[]{:S(2)}) async-start(bf16[32,8,2048]{2,1,0:T(8,128)(2,1)} %bitcast.40), calls=%async_computation | async-start | bytes 2097152 | tf_op jit(solution)/shard_map/all_to_all | solution.py:190
  379.8 43.8 %all-gather.18.cloned.1.call-done = bf16[1,2048,512]{2,1,0:T(8,128)(2,1)} async-done(((bf16[1,128,512]{2,1,0:T(8,128)(2,1)}), bf16[1,2048,512]{2,1,0:T(8,128)(2,1)}) %all-gather.18.cloned.1.call-update) | async-done | bytes 2097168 | tf_op jit(solution)/shard_map/all_gather | solution.py:186
  423.6 11.3 %all-to-all-done = bf16[32,8,2048]{2,1,0:T(8,128)(2,1)S(1)} async-done(((bf16[32,8,2048]{2,1,0:T(8,128)(2,1)}), bf16[32,8,2048]{2,1,0:T(8,128)(2,1)S(1)}, u32[]{:S(2)}, u32[]{:S(2)}) %all-to-all-start) | async-done | bytes 1048608 | tf_op jit(solution)/shard_map/all_to_all | solution.py:190
  434.9 2.3 fusion.32
  437.2 48.9 %all-gather.20.cloned.1.call-done = bf16[1,2048,512]{2,1,0:T(8,128)(2,1)} async-done(((bf16[1,128,512]{2,1,0:T(8,128)(2,1)}), bf16[1,2048,512]{2,1,0:T(8,128)(2,1)}) %all-gather.20.cloned.1.call-update) | async-done | bytes 2097168 | tf_op jit(solution)/shard_map/all_gather | solution.py:187
  486.2 65.3 %all-gather.22.cloned.1.call-done = bf16[1,512,2048]{2,1,0:T(8,128)(2,1)} async-done(((bf16[1,512,128]{2,1,0:T(8,128)(2,1)}), bf16[1,512,2048]{2,1,0:T(8,128)(2,1)}) %all-gather.22.cloned.1.call-update) | async-done | bytes 2097168 | tf_op jit(solution)/shard_map/all_gather | solution.py:188
  551.4 4.6 fusion.27
  556.0 13.9 %all-to-all-start.1 = ((bf16[32,8,2048]{2,1,0:T(8,128)(2,1)}), bf16[32,8,2048]{2,1,0:T(8,128)(2,1)S(1)}, u32[]{:S(2)}, u32[]{:S(2)}) async-start(bf16[32,8,2048]{2,1,0:T(8,128)(2,1)} %fusion.27), calls=%async_computation.1 | async-start | bytes 2097152 | tf_op jit(solution)/shard_map/all_to_all | solution.py:196
  569.9 55.7 %all-to-all-done.1 = bf16[32,8,2048]{2,1,0:T(8,128)(2,1)S(1)} async-done(((bf16[32,8,2048]{2,1,0:T(8,128)(2,1)}), bf16[32,8,2048]{2,1,0:T(8,128)(2,1)S(1)}, u32[]{:S(2)}, u32[]{:S(2)}) %all-to-all-start.1) | async-done | bytes 1048608 | tf_op jit(solution)/shard_map/all_to_all | solution.py:196
  (121 shorter events, 21.6 us)
Async XLA Ops:
  6.5 124.6 %copy-start = (f32[128]{0:T(128)S(1)}, f32[128]{0:T(128)}, u32[]{:S(2)}) copy-start(f32[128]{0:T(128)} %param.25) | copy-start | bytes 1540
  6.5 193.0 %all-gather.14.cloned.1.call-start = ((), (), s32[]{:S(2)}) async-start(), calls=%async_computation.3 | async-start | bytes 8912896 | tf_op jit(solution)/shard_map/all_gather | solution.py:21
  7.4 7.4 %collective-permute-start = (bf16[3,3072]{1,0:T(4,128)(2,1)S(1)}, bf16[3,3072]{1,0:T(4,128)(2,1)S(1)}, u32[]{:S(2)}, u32[]{:S(2)}) collective-permute-start(bf16[3,3072]{1,0:T(4,128)(2,1)S(1)} %slice_bitcast_fusion.3), channel_id=1, source_target_pairs={{0,32},{32,64},{64,96},{96,128},{128,160},{160,192},{192,224},{224... | collective-permute-start | bytes 55304 | tf_op jit(solution)/shard_map/ppermute | solution.py:16
  18.9 83.9 %copy-start.5 = (f32[16,8,8,128]{3,2,1,0:T(8,128)}, f32[16,8,8,128]{3,2,1,0:T(8,128)S(1)}, u32[]{:S(2)}) copy-start(f32[16,8,8,128]{3,2,1,0:T(8,128)S(1)} %copy.105) | copy-start | bytes 1572868
  100.5 2.3 copy-start.3
  105.1 4.5 copy-start.8
  105.1 26.0 %copy-start.9 = (s32[1,128,1]{1,2,0:T(1,128)S(1)}, s32[1,128,1]{1,2,0:T(1,128)}, u32[]{:S(2)}) copy-start(s32[1,128,1]{1,2,0:T(1,128)} %param.29) | copy-start | bytes 1540
  108.0 0.8 copy-start.1
  108.0 0.9 copy-start.2
  108.8 179.7 %all-gather.16.cloned.1.call-start = ((), (), s32[]{:S(2)}) async-start(), calls=%async_computation.4 | async-start | bytes 8912896 | tf_op jit(solution)/shard_map/all_gather | solution.py:21
  109.5 255.1 %all-gather.12.cloned.1.call-start = ((), (), s32[]{:S(2)}) async-start(), calls=%async_computation.2 | async-start | bytes 4325376 | tf_op jit(solution)/shard_map/all_gather | solution.py:163
  129.9 293.7 %all-gather.18.cloned.1.call-start = ((), (), s32[]{:S(2)}) async-start(), calls=%async_computation.5 | async-start | bytes 2228224 | tf_op jit(solution)/shard_map/all_gather | solution.py:186
  130.4 5.7 copy-start.6
  130.5 355.7 %all-gather.20.cloned.1.call-start = ((), (), s32[]{:S(2)}) async-start(), calls=%async_computation.6 | async-start | bytes 2228224 | tf_op jit(solution)/shard_map/all_gather | solution.py:187
  134.9 2.4 copy-start.4
  326.0 38.8 %copy-start.11 = (bf16[1,128,2048]{2,1,0:T(8,128)(2,1)S(1)}, bf16[1,128,2048]{2,1,0:T(8,128)(2,1)}, u32[]{:S(2)}) copy-start(bf16[1,128,2048]{2,1,0:T(8,128)(2,1)} %param.27) | copy-start | bytes 1572868
  326.0 38.8 %copy-start.12 = (bf16[1,128,1024]{2,1,0:T(8,128)(2,1)S(1)}, bf16[1,128,1024]{2,1,0:T(8,128)(2,1)}, u32[]{:S(2)}) copy-start(bf16[1,128,1024]{2,1,0:T(8,128)(2,1)} %param.24) | copy-start | bytes 786436
  364.8 3.3 copy-start.7
  370.7 64.3 %all-to-all-start = ((bf16[32,8,2048]{2,1,0:T(8,128)(2,1)}), bf16[32,8,2048]{2,1,0:T(8,128)(2,1)S(1)}, u32[]{:S(2)}, u32[]{:S(2)}) async-start(bf16[32,8,2048]{2,1,0:T(8,128)(2,1)} %bitcast.40), calls=%async_computation | async-start | bytes 2097152 | tf_op jit(solution)/shard_map/all_to_all | solution.py:190
  379.2 172.2 %all-gather.22.cloned.1.call-start = ((), (), s32[]{:S(2)}) async-start(), calls=%async_computation.7 | async-start | bytes 2228224 | tf_op jit(solution)/shard_map/all_gather | solution.py:188
  556.0 69.6 %all-to-all-start.1 = ((bf16[32,8,2048]{2,1,0:T(8,128)(2,1)}), bf16[32,8,2048]{2,1,0:T(8,128)(2,1)S(1)}, u32[]{:S(2)}, u32[]{:S(2)}) async-start(bf16[32,8,2048]{2,1,0:T(8,128)(2,1)} %fusion.27), calls=%async_computation.1 | async-start | bytes 2097152 | tf_op jit(solution)/shard_map/all_to_all | solution.py:196
  625.6 0.9 copy-start.10
Sparse Core Ops, SparseCore 0:
  108.9 90.6 all-gather.13
  202.6 85.8 all-gather.15
  290.6 73.9 all-gather.11
  367.4 56.0 all-gather.17
  426.4 59.6 all-gather.19
  489.0 62.3 all-gather.21
where the time goes:
time: 636 us; the launch traced here: 634 us
  waiting for transfers between devices  412 us (65%)
  other arithmetic  90.3 us (14%)
  matrix products  59 us (9%)
  starting transfers between devices  26.6 us (4%)
  blocking collectives  20.3 us (3%)
  between operations  14 us (2%)
  local copies, waits for them, and re-layouts  11.7 us (2%)
    all_gather x2, waiting for transfers between devices, carried_in(): everything = jax.tree.map(lambda part: lax.all_gather(part, axis), array)  149 us
    another operation x4, other arithmetic, on_device(): jax.scipy.linalg.solve_triangular(system, right, lower=True, unit_diagona...  78.7 us
    all_gather x1, waiting for transfers between devices, on_device(): lax.all_gather(w_down[0], 'ctx', axis=1, tiled=True)  65.3 us
    all_to_all x1, waiting for transfers between devices, on_device(): lax.all_to_all(answer.reshape(arrived.shape), 'exp', split_axis=0, concat...  55.7 us
    all_gather x1, waiting for transfers between devices, on_device(): lax.all_gather(w_up[0], 'ctx', axis=0, tiled=True)  48.9 us
    all_gather x1, waiting for transfers between devices, on_device(): lax.all_gather(w_gate[0], 'ctx', axis=0, tiled=True)  43.8 us
    all_gather x1, waiting for transfers between devices, on_device(): lax.all_gather(band, 'exp', axis=0, tiled=True)  35.7 us
    dot_general x22, matrix products, compose(): jnp.einsum('hde,hef->hdf', block_transit, state, precision=exact_mode)  34.3 us
  transfers between devices with their start and end apart: 9, of which 8 were waited for; matrix products, arithmetic and copies ran while one was open for 9% of the time, Pallas kernels for 0%

commit v1 on v0

v1 whole, which is shorter than its diff:
```python
import functools
import math

import jax
import jax.numpy as jnp
from jax import lax
from jax.experimental import pallas as pl
from jax.experimental.pallas import tpu as pltpu
from jax.sharding import PartitionSpec as P

MESH = pl.DeviceIdType.MESH
F32, BF16 = jnp.float32, jnp.bfloat16
NN, NT, TN = ((1,), (0,)), ((1,), (1,)), ((0,), (0,))
EPS = 1e-06
HD = 128
HALO = 16


def dot(a, b, dims=NN):
    return lax.dot_general(
        a.astype(BF16), b.astype(BF16), (dims, ((), ())), preferred_element_type=F32
    )


def silu(u):
    return u / (1.0 + jnp.exp(-u))


def copy_to(src, dst, send, recv, **where):
    return pltpu.make_async_remote_copy(
        src_ref=src,
        dst_ref=dst,
        send_sem=send,
        recv_sem=recv,
        device_id=where,
        device_id_type=MESH,
    )


def loop(low, high, body):
    lax.fori_loop(low, high, lambda i, c: (body(i), c)[1], 0)


def kernel(
    n_ctx,
    n_exp,
    side,
    qkv_ref,
    taps_ref,
    lgate_ref,
    beta_ref,
    z_ref,
    gain_ref,
    ow_ref,
    res_ref,
    post_ref,
    ids_ref,
    rw_ref,
    wg_ref,
    wu_ref,
    wd_ref,
    out_ref,
    halo,
    xs,
    keys,
    queries,
    decays,
    solved,
    ab_send,
    ab_recv,
    st_send,
    st_recv,
    qmap,
    lout,
    normed,
    colblk,
    wbuf,
    hidden,
    gate_full,
    up_full,
    down_full,
    outbound,
    arrived,
    answer,
    returned,
    halo_s,
    halo_r,
    col_s,
    col_r,
    band_s,
    band_r,
    core_s,
    core_r,
    ab_s,
    ab_r,
    st_s,
    st_r,
    w1_s,
    w1_r,
    w2_s,
    w2_r,
    out_s,
    out_r,
    back_s,
    back_r,
):
    ctx, exp = lax.axis_index("ctx"), lax.axis_index("exp")
    row, col = ctx // side, ctx % side
    tokens, width = qkv_ref.shape
    heads = width // (3 * HD)
    inner = heads * HD
    model = res_ref.shape[1]
    halfm = model // 2
    lanes = ow_ref.shape[1]
    slab = ow_ref.shape[0]
    cap = outbound.shape[1] // 2
    wrows = wg_ref.shape[0]
    sibling = exp + 1 - 2 * (exp % 2)
    half_in = inner // 2
    mine = pl.ds(pl.multiple_of((exp % 2) * half_in, half_in), half_in)
    theirs = pl.ds(pl.multiple_of((1 - exp % 2) * half_in, half_in), half_in)

    barrier = pltpu.get_barrier_semaphore()

    def greet_ctx(d):
        pl.semaphore_signal(
            barrier, inc=1, device_id={"ctx": (ctx + d) % n_ctx}, device_id_type=MESH
        )

    def greet_exp(d):
        pl.semaphore_signal(
            barrier, inc=1, device_id={"exp": (exp + d) % n_exp}, device_id_type=MESH
        )

    loop(1, n_ctx, greet_ctx)
    loop(1, n_exp, greet_exp)
    pl.semaphore_wait(barrier, n_ctx + n_exp - 2)

    halo_copy = copy_to(
        qkv_ref.at[pl.ds(tokens - HALO, HALO), :],
        halo,
        halo_s.at[0],
        halo_r.at[0],
        ctx=(ctx + 1) % n_ctx,
    )
    halo_copy.start()
    my_slab = pl.ds(pl.multiple_of(exp * slab, slab), slab)

    def col_copy(d):
        return copy_to(
            ow_ref, colblk.at[my_slab, :], col_s.at[d], col_r.at[d], exp=(exp + d) % n_exp
        )

    loop(1, n_exp, lambda d: col_copy(d).start())
    colblk[my_slab, :] = ow_ref[...]

    def along_x(d):
        return row * side + (col + d) % side

    def along_y(d):
        return ((row + d) % side) * side + col

    def w1_copies(d):
        return (
            copy_to(wg_ref, gate_full.at[row, col], w1_s.at[0, d], w1_r.at[0, d], ctx=along_x(d)),
            copy_to(wu_ref, up_full.at[row, col], w1_s.at[1, d], w1_r.at[1, d], ctx=along_y(d)),
            copy_to(
                wd_ref.at[pl.ds(0, wd_ref.shape[0] // 2), :],
                down_full.at[0, row, col],
                w1_s.at[2, d],
                w1_r.at[2, d],
                ctx=along_x(d),
            ),
            copy_to(
                wd_ref.at[pl.ds(wd_ref.shape[0] // 2, wd_ref.shape[0] // 2), :],
                down_full.at[1, row, col],
                w1_s.at[3, d],
                w1_r.at[3, d],
                ctx=along_y(d),
            ),
        )

    def w2_copies(d):
        return (
            copy_to(
                gate_full.at[row], gate_full.at[row], w2_s.at[0, d], w2_r.at[0, d], ctx=along_y(d)
            ),
            copy_to(
                up_full.at[:, col], up_full.at[:, col], w2_s.at[1, d], w2_r.at[1, d], ctx=along_x(d)
            ),
            copy_to(
                down_full.at[0, row],
                down_full.at[0, row],
                w2_s.at[2, d],
                w2_r.at[2, d],
                ctx=along_y(d),
            ),
            copy_to(
                down_full.at[1, :, col],
                down_full.at[1, :, col],
                w2_s.at[3, d],
                w2_r.at[3, d],
                ctx=along_x(d),
            ),
        )

    for d in range(1, side):
        for c in w1_copies(d):
            c.start()
    gate_full[row, col] = wg_ref[...]
    up_full[row, col] = wu_ref[...]
    down_full[0, row, col] = wd_ref[: wd_ref.shape[0] // 2, :]
    down_full[1, row, col] = wd_ref[wd_ref.shape[0] // 2 :, :]

    xs[8:, :] = qkv_ref[...].astype(F32)
    tri_r = lax.broadcasted_iota(jnp.int32, (tokens, tokens), 0)
    tri_c = lax.broadcasted_iota(jnp.int32, (tokens, tokens), 1)
    causal = tri_r >= tri_c
    strict = tri_r > tri_c
    eye = (tri_r == tri_c).astype(F32)
    growth_col = lax.dot_general(
        causal.astype(F32),
        lgate_ref[...],
        (NN, ((), ())),
        preferred_element_type=F32,
        precision=lax.Precision.HIGHEST,
    )
    last = growth_col[tokens - 1 :, :]
    strength = beta_ref[...]
    halo_copy.wait()
    xs[:8, :] = jnp.where(ctx > 0, halo[...].astype(F32)[HALO - 8 :, :], 0.0)
    taps = taps_ref[...].astype(F32)

    def active(block):
        at = slice(block * HD, (block + 1) * HD)
        total = xs[5 : 5 + tokens, at] * taps[0:1, at]
        for j in range(1, 4):
            total = total + xs[5 + j : 5 + j + tokens, at] * taps[j : j + 1, at]
        return silu(total)

    def unit(rows):
        return rows * lax.rsqrt(jnp.sum(rows * rows, axis=-1, keepdims=True) + EPS)

    lowers = []
    for h in range(heads):
        q = unit(active(h)) * HD ** (-0.5)
        k = unit(active(heads + h))
        queries[h] = q
        keys[h] = k
        gc = growth_col[:, h : h + 1]
        gr = jnp.sum(gc * eye, axis=0, keepdims=True)
        decay = jnp.where(causal, jnp.exp(jnp.where(causal, gc - gr, 0.0)), 0.0)
        decays[h] = decay
        kk = dot(k, k, NT)
        lowers.append(jnp.where(strict, strength[:, h : h + 1] * decay * kk, 0.0))

    def same(size):
        return tri_r // size == tri_c // size

    base = 16
    near = same(base)
    power = [jnp.where(near, l, 0.0) for l in lowers]
    inv = [eye - p for p in power]
    for _ in range(3):
        power = [dot(p, p) for p in power]
        inv = [x + dot(x, p) for x, p in zip(inv, power)]
    size = base
    while size < tokens:
        ring = jnp.logical_and(same(2 * size), jnp.logical_not(same(size)))
        mid = [dot(jnp.where(ring, l, 0.0), x) for l, x in zip(lowers, inv)]
        inv = [x - dot(x, m) for x, m in zip(inv, mid)]
        size *= 2

    def col_wait(d):
        c = col_copy(d)
        c.wait_send()
        c.wait_recv()

    loop(1, n_exp, col_wait)

    def band_copy(d):
        return copy_to(
            colblk.at[mine, :],
            wbuf.at[ctx, mine, :],
            band_s.at[d],
            band_r.at[d],
            ctx=(ctx + d) % n_ctx,
        )

    loop(1, n_ctx, lambda d: band_copy(d).start())
    wbuf[ctx] = colblk[...]

    for h in range(heads):
        b = strength[:, h : h + 1]
        gc = growth_col[:, h : h + 1]
        k = keys[h]
        v = active(2 * heads + h)
        rhs = jnp.concatenate([(b * jnp.exp(gc)) * k, b * v], axis=1)
        sol = dot(inv[h], rhs).astype(BF16)
        solved[h] = sol
        kept = jnp.exp(last[:, h : h + 1] - gc) * k
        both = dot(sol, kept, TN)
        at = (jnp.exp(last[:, h : h + 1]) * eye - both[:HD, :]).astype(BF16)
        bt = both[HD:, :].astype(BF16)
        ab_send[2 * h, :HD, :] = at
        ab_send[2 * h + 1, :HD, :] = at
        ab_send[2 * h, HD:, :] = bt[: HD // 2, :]
        ab_send[2 * h + 1, HD:, :] = bt[HD // 2 :, :]

    def ab_copy(d):
        to = (ctx + d) % n_ctx
        return copy_to(ab_send.at[to], ab_recv.at[ctx], ab_s.at[d], ab_r.at[d], ctx=to)

    loop(1, n_ctx, lambda d: ab_copy(d).start())
    ab_recv[ctx] = ab_send[ctx]

    for h in range(heads):
        gc = growth_col[:, h : h + 1]
        q = queries[h]
        qk = decays[h] * dot(q, keys[h], NT)
        both = dot(qk, solved[h])
        qmap[h] = (jnp.exp(gc) * q - both[:, :HD]).astype(BF16)
        lout[h] = both[:, HD:]

    def ab_wait(d):
        c = ab_copy(d)
        c.wait_send()
        c.wait_recv()

    loop(1, n_ctx, ab_wait)
    half = HD // 2
    state = jnp.zeros((half, HD), F32)
    for c in range(n_ctx):
        high = state.astype(BF16)
        st_send[c] = high
        if c < n_ctx - 1:
            low = (state - high.astype(F32)).astype(BF16)
            parts = dot(jnp.concatenate([high, low], axis=0), ab_recv[c, :HD, :])
            state = parts[:half] + parts[half:] + ab_recv[c, HD:, :].astype(F32)

    def st_copy(d):
        to = (ctx + d) % n_ctx
        return copy_to(st_send.at[to], st_recv.at[ctx], st_s.at[d], st_r.at[d], ctx=to)

    loop(1, n_ctx, lambda d: st_copy(d).start())
    st_recv[ctx] = st_send[ctx]

    def core_copy(d):
        src = (ctx + n_ctx - d) % n_ctx
        return copy_to(
            wbuf.at[src, mine, :],
            wbuf.at[src, mine, :],
            core_s.at[d],
            core_r.at[d],
            exp=sibling,
        )

    def forward(d):
        c = band_copy(d)
        c.wait_send()
        c.wait_recv()
        core_copy(d).start()

    loop(1, n_ctx, forward)

    def st_wait(d):
        c = st_copy(d)
        c.wait_send()
        c.wait_recv()

    loop(1, n_ctx, st_wait)

    for d in range(1, side):
        for c in w1_copies(d):
            c.wait_send()
            c.wait_recv()
    for d in range(1, side):
        for c in w2_copies(d):
            c.start()

    gain = gain_ref[...]
    for h in range(heads):
        st = jnp.concatenate([st_recv[2 * h], st_recv[2 * h + 1]], axis=0)
        core = dot(qmap[h], st, NT) + lout[h]
        scale = lax.rsqrt(jnp.mean(core * core, axis=-1, keepdims=True) + EPS)
        z = z_ref[:, h * HD : (h + 1) * HD].astype(F32)
        normed[:, h * HD : (h + 1) * HD] = (core * scale * gain * silu(z)).astype(BF16)

    def core_wait(d):
        c = core_copy(d)
        c.wait_send()
        c.wait_recv()

    loop(1, n_ctx, core_wait)

    squares = jnp.zeros((tokens, 1), F32)
    act = normed[...]
    for j in range(n_ctx):
        at = slice(j * lanes, (j + 1) * lanes)
        hid = (res_ref[:, at].astype(F32) + dot(act, wbuf[j])).astype(BF16)
        hidden[:, at] = hid
        hid = hid.astype(F32)
        squares = squares + jnp.sum(hid * hid, axis=-1, keepdims=True)
    scale = lax.rsqrt(squares / model + EPS)
    routed_in = (hidden[...].astype(F32) * scale * post_ref[...]).astype(BF16)

    ids = ids_ref[...]
    member = lax.broadcasted_iota(jnp.int32, (tokens, n_exp), 1) == ids
    member = member.astype(F32)
    ranks = dot(causal.astype(F32), member)
    slot = jnp.sum(ranks * member, axis=1, keepdims=True).astype(jnp.int32) - 1
    first = ids * (2 * cap) + slot
    places = lax.broadcasted_iota(jnp.int32, (tokens, 2 * cap * n_exp), 1)
    pick_low = (places == first).astype(F32).astype(BF16)
    pick_high = (places == first + cap).astype(F32).astype(BF16)
    sent = dot(pick_low, routed_in[:, :halfm], TN) + dot(pick_high, routed_in[:, halfm:], TN)
    outbound[...] = sent.astype(BF16).reshape(outbound.shape)

    def out_copy(d):
        to = (exp + d) % n_exp
        return copy_to(outbound.at[to], arrived.at[exp], out_s.at[d], out_r.at[d], exp=to)

    loop(1, n_exp, lambda d: out_copy(d).start())
    arrived[exp] = outbound[exp]

    for d in range(1, side):
        for c in w2_copies(d):
            c.wait_send()
            c.wait_recv()

    def out_wait(d):
        c = out_copy(d)
        c.wait_send()
        c.wait_recv()

    loop(1, n_exp, out_wait)

    ff = wg_ref.shape[1]
    came = arrived[...].astype(F32)
    rows_in = jnp.concatenate(
        [
            came[:, :cap, :].reshape(n_exp * cap, halfm),
            came[:, cap:, :].reshape(n_exp * cap, halfm),
        ],
        axis=1,
    ).astype(BF16)
    gate_part = dot(rows_in, gate_full[...].reshape(model, ff))
    up_part = dot(rows_in, up_full[...].reshape(model, ff))
    activated = (silu(gate_part) * up_part).astype(BF16)
    blocks = n_ctx // 2
    for j in range(blocks):
        parts = []
        for i in (j, j + blocks):
            down = jnp.concatenate(
                [down_full[0, i // side, i % side], down_full[1, i // side, i % side]], axis=0
            )
            parts.append(dot(activated, down).reshape(n_exp, cap, lanes))
        answer[:, :, j * lanes : (j + 1) * lanes] = jnp.concatenate(parts, axis=1).astype(BF16)

    def back_copy(d):
        to = (exp + d) % n_exp
        return copy_to(answer.at[to], returned.at[exp], back_s.at[d], back_r.at[d], exp=to)

    loop(1, n_exp, lambda d: back_copy(d).start())
    returned[exp] = answer[exp]

    def back_wait(d):
        c = back_copy(d)
        c.wait_send()
        c.wait_recv()

    loop(1, n_exp, back_wait)

    back = returned[...].reshape(2 * cap * n_exp, halfm)
    weight = rw_ref[...]
    for pick, at in ((pick_low, slice(0, halfm)), (pick_high, slice(halfm, model))):
        fetched = dot(pick, back)
        out_ref[:, at] = (hidden[:, at].astype(F32) + weight * fetched).astype(BF16)


def on_device(n_ctx, n_exp, *args):
    (qkv, taps, lgate, beta, z, gain, ow, res, post, ids, rw, wg, wu, wd) = args
    tokens, width = qkv.shape[1:]
    heads = lgate.shape[2]
    model = res.shape[2]
    ff = wg.shape[2]
    side = math.isqrt(n_ctx)
    cap = 2 * ids.shape[2] * tokens // n_exp
    inner = heads * HD
    lanes = ow.shape[1]
    sem = pltpu.SemaphoreType.DMA
    slots = (n_exp, 2 * cap, model // 2)
    scratch = [
        pltpu.VMEM((HALO, width), BF16),
        pltpu.VMEM((8 + tokens, width), F32),
        pltpu.VMEM((heads, tokens, HD), F32),
        pltpu.VMEM((heads, tokens, HD), F32),
        pltpu.VMEM((heads, tokens, tokens), F32),
        pltpu.VMEM((heads, tokens, 2 * HD), BF16),
        pltpu.VMEM((n_ctx, HD + HD // 2, HD), BF16),
        pltpu.VMEM((n_ctx, HD + HD // 2, HD), BF16),
        pltpu.VMEM((n_ctx, HD // 2, HD), BF16),
        pltpu.VMEM((n_ctx, HD // 2, HD), BF16),
        pltpu.VMEM((heads, tokens, HD), BF16),
        pltpu.VMEM((heads, tokens, HD), F32),
        pltpu.VMEM((tokens, inner), BF16),
        pltpu.VMEM((inner, lanes), BF16),
        pltpu.VMEM((n_ctx, inner, lanes), BF16),
        pltpu.VMEM((tokens, model), BF16),
        pltpu.VMEM((side, side, model // n_ctx, ff), BF16),
        pltpu.VMEM((side, side, model // n_ctx, ff), BF16),
        pltpu.VMEM((2, side, side, ff // 2, lanes), BF16),
        pltpu.VMEM(slots, BF16),
        pltpu.VMEM(slots, BF16),
        pltpu.VMEM(slots, BF16),
        pltpu.VMEM(slots, BF16),
        sem((1,)),
        sem((1,)),
        sem((n_exp,)),
        sem((n_exp,)),
        sem((n_ctx,)),
        sem((n_ctx,)),
        sem((n_ctx,)),
        sem((n_ctx,)),
        sem((n_ctx,)),
        sem((n_ctx,)),
        sem((n_ctx,)),
        sem((n_ctx,)),
        sem((4, side)),
        sem((4, side)),
        sem((4, side)),
        sem((4, side)),
        sem((n_exp,)),
        sem((n_exp,)),
        sem((n_exp,)),
        sem((n_exp,)),
    ]
    out = pl.pallas_call(
        functools.partial(kernel, n_ctx, n_exp, side),
        out_shape=jax.ShapeDtypeStruct((tokens, model), BF16),
        in_specs=[pl.BlockSpec(memory_space=pltpu.VMEM)] * 14,
        out_specs=pl.BlockSpec(memory_space=pltpu.VMEM),
        scratch_shapes=scratch,
        compiler_params=pltpu.CompilerParams(
            collective_id=0, has_side_effects=True, vmem_limit_bytes=48 * 2**20
        ),
    )(
        qkv[0],
        taps,
        lgate[0],
        beta[0],
        z[0],
        gain[None],
        ow,
        res[0],
        post[None],
        ids[0],
        rw[0],
        wg[0],
        wu[0],
        wd[0],
    )
    return out[None]


def solution(mesh):
    placed = (
        P("exp", "ctx", None),
        P(),
        P("exp", "ctx", None),
        P("exp", "ctx", None),
        P("exp", "ctx", None),
        P(),
        P("exp", "ctx"),
        P("exp", "ctx", None),
        P(),
        P("exp", "ctx", None),
        P("exp", "ctx", None),
        P("exp", "ctx", None),
        P("exp", "ctx", None),
        P("exp", None, "ctx"),
    )
    return jax.shard_map(
        functools.partial(on_device, mesh.shape["ctx"], mesh.shape["exp"]),
        mesh=mesh,
        in_specs=placed,
        out_specs=P("exp", "ctx", None),
        check_vma=False,
    )
```

time: 636 us -> 196 us (0.31)
  waiting for transfers between devices: 412 us -> 0 us
  Pallas kernels: 0 us -> 183 us
  other arithmetic: 90.3 us -> 0 us
  matrix products: 59 us -> 0 us
  starting transfers between devices: 26.6 us -> 0 us
  blocking collectives: 20.3 us -> 0 us
  between operations: 14 us -> 0.06 us
    all_gather x6 -> x0, waiting for transfers between devices: 343 us -> none  [the longest x2 149 us: carried_in(): everything = jax.tree.map(lambda part: lax.all_gather(part, axis), array)]
    pallas_call x0 -> x1, Pallas kernels: none -> 183 us  [on_device(): pl.pallas_call(functools.partial(kernel, n_ctx, n_exp, side), out_shape=j...]
    another operation x6 -> x0, other arithmetic: 79.4 us -> none  [the longest x4 78.7 us: on_device(): jax.scipy.linalg.solve_triangular(system, right, lower=True, unit_diagona...]
    all_to_all x2 -> x0, waiting for transfers between devices: 67 us -> none  [the longest x1 55.7 us: on_device(): lax.all_to_all(answer.reshape(arrived.shape), 'exp', split_axis=0, concat...]
    dot_general x33 -> x0, matrix products: 57.9 us -> none  [the longest x22 34.3 us: compose(): jnp.einsum('hde,hef->hdf', block_transit, state, precision=exact_mode)]
    all_to_all x2 -> x0, starting transfers between devices: 22.4 us -> none  [the longest x1 13.9 us: on_device(): lax.all_to_all(answer.reshape(arrived.shape), 'exp', split_axis=0, concat...]
    all_gather x1 -> x0, blocking collectives: 20.3 us -> none  [on_device(): band = lax.all_gather(out_weight, 'ctx', axis=1, tiled=True)]
  transfers between devices with their start and end apart: 9 -> 0, of which waited for: 8 -> 0; matrix products, arithmetic and copies ran while one was open for 9% -> 0% of each run, Pallas kernels for 0% -> 0%
where the time goes in v1:
time: 196 us; the launch traced here: 193 us
  Pallas kernels  183 us (93%)
  local copies, waits for them, and re-layouts  10.2 us (5%)
    pallas_call x1, Pallas kernels, on_device(): pl.pallas_call(functools.partial(kernel, n_ctx, n_exp, side), out_shape=j...  183 us
    unnamed x23, local copies, waits for them, and re-layouts  8.7 us

profile of v1, /device:TPU:1, one launch (start us, length us, event | category | flops | bytes accessed | tf_op | source)
XLA Modules:
  0.0 192.9 jit_solution(3681366216723770203)
XLA Ops:
  0.0 0.0 copy-start.2
  0.0 0.8 copy.15
  0.8 0.8 copy.16
  1.6 0.8 copy.17.ids_ref
  2.4 0.0 copy-start.6
  2.4 0.0 copy-start.9
  2.4 0.8 copy.18.rw_ref
  3.2 0.0 copy-done.2
  3.2 0.0 copy-done.6
  3.2 0.0 copy-done.9
  3.2 0.0 copy-start
  3.2 1.1 copy-done
  4.3 0.0 copy-start.1
  4.3 1.0 copy-done.1
  5.4 0.0 copy-start.3
  5.4 0.9 copy-done.3
  6.3 0.0 copy-start.4
  6.3 0.9 copy-done.4
  7.2 0.0 copy-start.5
  7.2 0.9 copy-done.5
  8.1 0.0 copy-start.7
  8.1 0.7 copy-done.7
  8.8 0.0 copy-start.8
  8.8 0.7 copy-done.8
  9.5 182.6 %shard_map.136 = bf16[128,2048]{1,0:T(8,128)(2,1)S(1)} custom-call(bf16[128,3072]{1,0:T(8,128)(2,1)S(1)} %bitcast.14, bf16[4,3072]{1,0:T(4,128)(2,1)S(1)} %copy-done.6, f32[128,8]{1,0:T(8,128)S(1)} %bitcast.17, f32[128,8]{1,0:T(8,128)S(1)} %bitcast.18, bf16[128,1024]{1,0:T(8,128)(2,1)S(1)} %bitcast.16, f32[1,128]{1,0:T(1,128)S(1)} %bitcast.23, ...), custom_call_target="tpu_custom_call" | custom-call | tf_op jit(solution)/shard_map/pallas_call | solution.py:538
  192.1 0.8 copy.20
Async XLA Ops:
  0.0 3.2 %copy-start.2 = (bf16[1,128,1024]{2,1,0:T(8,128)(2,1)S(1)}, bf16[1,128,1024]{2,1,0:T(8,128)(2,1)}, u32[]{:S(2)}) copy-start(bf16[1,128,1024]{2,1,0:T(8,128)(2,1)} %param.18) | copy-start | bytes 786436
  2.4 0.8 copy-start.6
  2.4 0.8 copy-start.9
  3.2 1.1 copy-start
  4.3 1.0 copy-start.1
  5.4 0.9 copy-start.3
  6.3 0.9 copy-start.4
  7.2 0.9 copy-start.5
  8.1 0.7 copy-start.7
  8.8 0.7 copy-start.8

commit v2 on v1

--- a/solution.py
+++ b/solution.py
@@ -45,6 +45,21 @@
     n_ctx,
     n_exp,
     side,
+    qkv_hbm,
+    taps_hbm,
+    lgate_hbm,
+    beta_hbm,
+    z_hbm,
+    gain_hbm,
+    ow_hbm,
+    res_hbm,
+    post_hbm,
+    ids_hbm,
+    rw_hbm,
+    wg_ref,
+    wu_ref,
+    wd_ref,
+    out_ref,
     qkv_ref,
     taps_ref,
     lgate_ref,
@@ -56,10 +71,6 @@
     post_ref,
     ids_ref,
     rw_ref,
-    wg_ref,
-    wu_ref,
-    wd_ref,
-    out_ref,
     halo,
     xs,
     keys,
@@ -83,12 +94,16 @@
     arrived,
     answer,
     returned,
+    load_s,
+    own_s,
     halo_s,
     halo_r,
     col_s,
     col_r,
-    band_s,
-    band_r,
+    band1_s,
+    band1_r,
+    band2_s,
+    band2_r,
     core_s,
     core_r,
     ab_s,
@@ -115,10 +130,10 @@
     slab = ow_ref.shape[0]
     cap = outbound.shape[1] // 2
     wrows = wg_ref.shape[0]
-    sibling = exp + 1 - 2 * (exp % 2)
-    half_in = inner // 2
-    mine = pl.ds(pl.multiple_of((exp % 2) * half_in, half_in), half_in)
-    theirs = pl.ds(pl.multiple_of((1 - exp % 2) * half_in, half_in), half_in)
+    chip, core = exp // 2, exp % 2
+    chips = n_exp // 2
+    sibling = exp + 1 - 2 * core
+    composer = ctx % 2 == core
 
     barrier = pltpu.get_barrier_semaphore()
 
@@ -134,6 +149,45 @@
 
     loop(1, n_ctx, greet_ctx)
     loop(1, n_exp, greet_exp)
+    loads = [
+        pltpu.make_async_copy(src, dst, load_s.at[i])
+        for i, (src, dst) in enumerate(
+            (
+                (qkv_hbm, qkv_ref),
+                (taps_hbm, taps_ref),
+                (lgate_hbm, lgate_ref),
+                (beta_hbm, beta_ref),
+                (ow_hbm, ow_ref),
+                (z_hbm, z_ref),
+                (gain_hbm, gain_ref),
+                (res_hbm, res_ref),
+                (post_hbm, post_ref),
+                (ids_hbm, ids_ref),
+                (rw_hbm, rw_ref),
+            )
+        )
+    ]
+    for c in loads:
+        c.start()
+    owns = [
+        pltpu.make_async_copy(src, dst, own_s.at[i])
+        for i, (src, dst) in enumerate(
+            (
+                (wg_ref, gate_full.at[row, col]),
+                (wu_ref, up_full.at[row, col]),
+                (wd_ref.at[pl.ds(0, wd_ref.shape[0] // 2), :], down_full.at[0, row, col]),
+                (
+                    wd_ref.at[pl.ds(wd_ref.shape[0] // 2, wd_ref.shape[0] // 2), :],
+                    down_full.at[1, row, col],
+                ),
+            )
+        )
+    ]
+    for c in owns:
+        c.start()
+    for c in loads[:5]:
+        c.wait()
+    xs[8:, :] = qkv_ref[...].astype(F32)
     pl.semaphore_wait(barrier, n_ctx + n_exp - 2)
 
     halo_copy = copy_to(
@@ -144,15 +198,14 @@
         ctx=(ctx + 1) % n_ctx,
     )
     halo_copy.start()
-    my_slab = pl.ds(pl.multiple_of(exp * slab, slab), slab)
 
     def col_copy(d):
         return copy_to(
-            ow_ref, colblk.at[my_slab, :], col_s.at[d], col_r.at[d], exp=(exp + d) % n_exp
-        )
-
-    loop(1, n_exp, lambda d: col_copy(d).start())
-    colblk[my_slab, :] = ow_ref[...]
+            ow_ref, colblk.at[chip], col_s.at[d], col_r.at[d], exp=(exp + 2 * d) % n_exp
+        )
+
+    loop(1, chips, lambda d: col_copy(d).start())
+    colblk[chip] = ow_ref[...]
 
     def along_x(d):
         return row * side + (col + d) % side
@@ -207,26 +260,27 @@
     for d in range(1, side):
         for c in w1_copies(d):
             c.start()
-    gate_full[row, col] = wg_ref[...]
-    up_full[row, col] = wu_ref[...]
-    down_full[0, row, col] = wd_ref[: wd_ref.shape[0] // 2, :]
-    down_full[1, row, col] = wd_ref[wd_ref.shape[0] // 2 :, :]
-
-    xs[8:, :] = qkv_ref[...].astype(F32)
+
     tri_r = lax.broadcasted_iota(jnp.int32, (tokens, tokens), 0)
     tri_c = lax.broadcasted_iota(jnp.int32, (tokens, tokens), 1)
     causal = tri_r >= tri_c
     strict = tri_r > tri_c
     eye = (tri_r == tri_c).astype(F32)
-    growth_col = lax.dot_general(
-        causal.astype(F32),
+    growth_row = lax.dot_general(
         lgate_ref[...],
+        (tri_r <= tri_c).astype(F32),
         (NN, ((), ())),
         preferred_element_type=F32,
         precision=lax.Precision.HIGHEST,
     )
-    last = growth_col[tokens - 1 :, :]
-    strength = beta_ref[...]
+
+    def column(line):
+        return jnp.sum(line * eye, axis=1, keepdims=True)
+
+    growth = [growth_row[h : h + 1, :] for h in range(heads)]
+    growth_col = [column(g) for g in growth]
+    last = [g[:, tokens - 1 :] for g in growth]
+    strength = [column(beta_ref[h : h + 1, :]) for h in range(heads)]
     halo_copy.wait()
     xs[:8, :] = jnp.where(ctx > 0, halo[...].astype(F32)[HALO - 8 :, :], 0.0)
     taps = taps_ref[...].astype(F32)
@@ -247,12 +301,11 @@
         k = unit(active(heads + h))
         queries[h] = q
         keys[h] = k
-        gc = growth_col[:, h : h + 1]
-        gr = jnp.sum(gc * eye, axis=0, keepdims=True)
+        gc, gr = growth_col[h], growth[h]
         decay = jnp.where(causal, jnp.exp(jnp.where(causal, gc - gr, 0.0)), 0.0)
         decays[h] = decay
         kk = dot(k, k, NT)
-        lowers.append(jnp.where(strict, strength[:, h : h + 1] * decay * kk, 0.0))
+        lowers.append(jnp.where(strict, strength[h] * decay * kk, 0.0))
 
     def same(size):
         return tri_r // size == tri_c // size
@@ -276,135 +329,175 @@
         c.wait_send()
         c.wait_recv()
 
-    loop(1, n_exp, col_wait)
-
-    def band_copy(d):
-        return copy_to(
-            colblk.at[mine, :],
-            wbuf.at[ctx, mine, :],
-            band_s.at[d],
-            band_r.at[d],
-            ctx=(ctx + d) % n_ctx,
-        )
-
-    loop(1, n_ctx, lambda d: band_copy(d).start())
-    wbuf[ctx] = colblk[...]
+    loop(1, chips, col_wait)
+    fore, rear = pl.ds(0, chips // 2), pl.ds(chips // 2, chips // 2)
+
+    def band1_copies(d):
+        return (
+            copy_to(
+                colblk.at[fore],
+                wbuf.at[row, col, fore, core],
+                band1_s.at[0, d],
+                band1_r.at[0, d],
+                ctx=along_x(d),
+            ),
+            copy_to(
+                colblk.at[rear],
+                wbuf.at[row, col, rear, core],
+                band1_s.at[1, d],
+                band1_r.at[1, d],
+                ctx=along_y(d),
+            ),
+        )
+
+    def band2_copies(d):
+        ahead, behind = wbuf.at[row, :, fore, core], wbuf.at[:, col, rear, core]
+        return (
+            copy_to(ahead, ahead, band2_s.at[0, d], band2_r.at[0, d], ctx=along_y(d)),
+            copy_to(behind, behind, band2_s.at[1, d], band2_r.at[1, d], ctx=along_x(d)),
+        )
+
+    for d in range(1, side):
+        for c in band1_copies(d):
+            c.start()
+    wbuf[row, col, :, core] = colblk[...]
 
     for h in range(heads):
-        b = strength[:, h : h + 1]
-        gc = growth_col[:, h : h + 1]
+        b = strength[h]
+        gc = growth_col[h]
         k = keys[h]
         v = active(2 * heads + h)
         rhs = jnp.concatenate([(b * jnp.exp(gc)) * k, b * v], axis=1)
         sol = dot(inv[h], rhs).astype(BF16)
         solved[h] = sol
-        kept = jnp.exp(last[:, h : h + 1] - gc) * k
+        kept = jnp.exp(last[h] - gc) * k
         both = dot(sol, kept, TN)
-        at = (jnp.exp(last[:, h : h + 1]) * eye - both[:HD, :]).astype(BF16)
+        at = (jnp.exp(last[h]) * eye - both[:HD, :]).astype(BF16)
         bt = both[HD:, :].astype(BF16)
-        ab_send[2 * h, :HD, :] = at
-        ab_send[2 * h + 1, :HD, :] = at
-        ab_send[2 * h, HD:, :] = bt[: HD // 2, :]
-        ab_send[2 * h + 1, HD:, :] = bt[HD // 2 :, :]
-
-    def ab_copy(d):
-        to = (ctx + d) % n_ctx
-        return copy_to(ab_send.at[to], ab_recv.at[ctx], ab_s.at[d], ab_r.at[d], ctx=to)
-
-    loop(1, n_ctx, lambda d: ab_copy(d).start())
-    ab_recv[ctx] = ab_send[ctx]
+        ab_send[h, :HD, :] = at
+        ab_send[h, HD:, :] = bt
+
+    def ab_copy(h):
+        to = 2 * h + core
+        return copy_to(ab_send.at[h], ab_recv.at[ctx], ab_s.at[h], ab_r.at[ctx], ctx=to)
+
+    def ab_arrival(src):
+        return copy_to(ab_send.at[0], ab_recv.at[src], ab_s.at[0], ab_r.at[src], ctx=src)
+
+    def unless(skip, body):
+        def step(i):
+            @pl.when(i != skip)
+            def _():
+                body(i)
+
+        return step
+
+    mine = jnp.where(composer, ctx // 2, n_ctx)
+    loop(0, heads, unless(mine, lambda h: ab_copy(h).start()))
+
+    @pl.when(composer)
+    def _():
+        ab_recv[ctx] = ab_send[ctx // 2]
 
     for h in range(heads):
-        gc = growth_col[:, h : h + 1]
+        gc = growth_col[h]
         q = queries[h]
         qk = decays[h] * dot(q, keys[h], NT)
         both = dot(qk, solved[h])
         qmap[h] = (jnp.exp(gc) * q - both[:, :HD]).astype(BF16)
         lout[h] = both[:, HD:]
 
-    def ab_wait(d):
-        c = ab_copy(d)
-        c.wait_send()
-        c.wait_recv()
-
-    loop(1, n_ctx, ab_wait)
-    half = HD // 2
-    state = jnp.zeros((half, HD), F32)
-    for c in range(n_ctx):
-        high = state.astype(BF16)
-        st_send[c] = high
-        if c < n_ctx - 1:
-            low = (state - high.astype(F32)).astype(BF16)
-            parts = dot(jnp.concatenate([high, low], axis=0), ab_recv[c, :HD, :])
-            state = parts[:half] + parts[half:] + ab_recv[c, HD:, :].astype(F32)
-
-    def st_copy(d):
-        to = (ctx + d) % n_ctx
-        return copy_to(st_send.at[to], st_recv.at[ctx], st_s.at[d], st_r.at[d], ctx=to)
-
-    loop(1, n_ctx, lambda d: st_copy(d).start())
-    st_recv[ctx] = st_send[ctx]
-
-    def core_copy(d):
-        src = (ctx + n_ctx - d) % n_ctx
+    for d in range(1, side):
+        for c in band1_copies(d):
+            c.wait_send()
+            c.wait_recv()
+    for d in range(1, side):
+        for c in band2_copies(d):
+            c.start()
+
+    def core_copies(d):
+        r, q = (row + side - d) % side, (col + side - d) % side
+        ahead, behind = wbuf.at[r, :, fore, core], wbuf.at[:, q, rear, core]
+        return (
+            copy_to(ahead, ahead, core_s.at[0, d], core_r.at[0, d], exp=sibling),
+            copy_to(behind, behind, core_s.at[1, d], core_r.at[1, d], exp=sibling),
+        )
+
+    for c in core_copies(0):
+        c.start()
+
+    def st_copy(to):
         return copy_to(
-            wbuf.at[src, mine, :],
-            wbuf.at[src, mine, :],
-            core_s.at[d],
-            core_r.at[d],
-            exp=sibling,
-        )
-
-    def forward(d):
-        c = band_copy(d)
-        c.wait_send()
-        c.wait_recv()
-        core_copy(d).start()
-
-    loop(1, n_ctx, forward)
-
-    def st_wait(d):
-        c = st_copy(d)
-        c.wait_send()
-        c.wait_recv()
-
-    loop(1, n_ctx, st_wait)
+            st_send.at[to], st_recv.at[ctx // 2], st_s.at[to], st_r.at[ctx // 2], ctx=to
+        )
+
+    @pl.when(composer)
+    def _():
+        loop(0, n_ctx, unless(ctx, lambda src: ab_arrival(src).wait_recv()))
+        state = jnp.zeros((HD, HD), F32)
+        for c in range(n_ctx):
+            high = state.astype(BF16)
+            st_send[c] = high
+            if c < n_ctx - 1:
+                low = (state - high.astype(F32)).astype(BF16)
+                parts = dot(jnp.concatenate([high, low], axis=0), ab_recv[c, :HD, :])
+                state = parts[:HD] + parts[HD:] + ab_recv[c, HD:, :].astype(F32)
+        loop(0, n_ctx, unless(ctx, lambda to: st_copy(to).start()))
+        st_recv[ctx // 2] = st_send[ctx]
+
+    for d in range(1, side):
+        for c, onward in zip(band2_copies(d), core_copies(d)):
+            c.wait_send()
+            c.wait_recv()
+            onward.start()
+
+    def st_arrival(h):
+        src = 2 * h + core
+        return copy_to(st_send.at[0], st_recv.at[h], st_s.at[0], st_r.at[h], ctx=src)
+
+    loop(0, heads, unless(mine, lambda h: st_arrival(h).wait_recv()))
+    loop(0, heads, unless(mine, lambda h: ab_copy(h).wait_send()))
+
+    @pl.when(composer)
+    def _():
+        loop(0, n_ctx, unless(ctx, lambda to: st_copy(to).wait_send()))
 
     for d in range(1, side):
         for c in w1_copies(d):
             c.wait_send()
             c.wait_recv()
+    for c in owns:
+        c.wait()
     for d in range(1, side):
         for c in w2_copies(d):
             c.start()
 
+    for c in loads[5:]:
+        c.wait()
     gain = gain_ref[...]
     for h in range(heads):
-        st = jnp.concatenate([st_recv[2 * h], st_recv[2 * h + 1]], axis=0)
-        core = dot(qmap[h], st, NT) + lout[h]
-        scale = lax.rsqrt(jnp.mean(core * core, axis=-1, keepdims=True) + EPS)
+        read = dot(qmap[h], st_recv[h], NT) + lout[h]
+        scale = lax.rsqrt(jnp.mean(read * read, axis=-1, keepdims=True) + EPS)
         z = z_ref[:, h * HD : (h + 1) * HD].astype(F32)
-        normed[:, h * HD : (h + 1) * HD] = (core * scale * gain * silu(z)).astype(BF16)
-
-    def core_wait(d):
-        c = core_copy(d)
-        c.wait_send()
-        c.wait_recv()
-
-    loop(1, n_ctx, core_wait)
+        normed[:, h * HD : (h + 1) * HD] = (read * scale * gain * silu(z)).astype(BF16)
+
+    for d in range(side):
+        for c in core_copies(d):
+            c.wait_send()
+            c.wait_recv()
 
     squares = jnp.zeros((tokens, 1), F32)
     act = normed[...]
     for j in range(n_ctx):
         at = slice(j * lanes, (j + 1) * lanes)
-        hid = (res_ref[:, at].astype(F32) + dot(act, wbuf[j])).astype(BF16)
+        hid = (res_ref[:, at].astype(F32) + dot(act, wbuf[j // side, j % side].reshape(inner, lanes))).astype(BF16)
         hidden[:, at] = hid
         hid = hid.astype(F32)
         squares = squares + jnp.sum(hid * hid, axis=-1, keepdims=True)
     scale = lax.rsqrt(squares / model + EPS)
     routed_in = (hidden[...].astype(F32) * scale * post_ref[...]).astype(BF16)
 
-    ids = ids_ref[...]
+    ids = column(ids_ref[...].astype(F32)).astype(jnp.int32)
     member = lax.broadcasted_iota(jnp.int32, (tokens, n_exp), 1) == ids
     member = member.astype(F32)
     ranks = dot(causal.astype(F32), member)
@@ -472,7 +565,7 @@
     loop(1, n_exp, back_wait)
 
     back = returned[...].reshape(2 * cap * n_exp, halfm)
-    weight = rw_ref[...]
+    weight = column(rw_ref[...])
     for pick, at in ((pick_low, slice(0, halfm)), (pick_high, slice(halfm, model))):
         fetched = dot(pick, back)
         out_ref[:, at] = (hidden[:, at].astype(F32) + weight * fetched).astype(BF16)
@@ -488,24 +581,42 @@
     cap = 2 * ids.shape[2] * tokens // n_exp
     inner = heads * HD
     lanes = ow.shape[1]
+    chips = n_exp // 2
     sem = pltpu.SemaphoreType.DMA
+    operands = (
+        qkv[0],
+        taps,
+        lgate[0].T,
+        beta[0].T,
+        z[0],
+        gain[None],
+        ow,
+        res[0],
+        post[None],
+        ids[0].T,
+        rw[0].T,
+        wg[0],
+        wu[0],
+        wd[0],
+    )
     slots = (n_exp, 2 * cap, model // 2)
-    scratch = [
+    scratch = [pltpu.VMEM(x.shape, x.dtype) for x in operands[:11]]
+    scratch += [
         pltpu.VMEM((HALO, width), BF16),
         pltpu.VMEM((8 + tokens, width), F32),
         pltpu.VMEM((heads, tokens, HD), F32),
         pltpu.VMEM((heads, tokens, HD), F32),
         pltpu.VMEM((heads, tokens, tokens), F32),
         pltpu.VMEM((heads, tokens, 2 * HD), BF16),
-        pltpu.VMEM((n_ctx, HD + HD // 2, HD), BF16),
-        pltpu.VMEM((n_ctx, HD + HD // 2, HD), BF16),
-        pltpu.VMEM((n_ctx, HD // 2, HD), BF16),
-        pltpu.VMEM((n_ctx, HD // 2, HD), BF16),
+        pltpu.VMEM((heads, 2 * HD, HD), BF16),
+        pltpu.VMEM((n_ctx, 2 * HD, HD), BF16),
+        pltpu.VMEM((n_ctx, HD, HD), BF16),
+        pltpu.VMEM((heads, HD, HD), BF16),
         pltpu.VMEM((heads, tokens, HD), BF16),
         pltpu.VMEM((heads, tokens, HD), F32),
         pltpu.VMEM((tokens, inner), BF16),
-        pltpu.VMEM((inner, lanes), BF16),
-        pltpu.VMEM((n_ctx, inner, lanes), BF16),
+        pltpu.VMEM((chips, ow.shape[0], lanes), BF16),
+        pltpu.VMEM((side, side, chips, 2, ow.shape[0], lanes), BF16),
         pltpu.VMEM((tokens, model), BF16),
         pltpu.VMEM((side, side, model // n_ctx, ff), BF16),
         pltpu.VMEM((side, side, model // n_ctx, ff), BF16),
@@ -514,18 +625,22 @@
         pltpu.VMEM(slots, BF16),
         pltpu.VMEM(slots, BF16),
         pltpu.VMEM(slots, BF16),
+        sem((11,)),
+        sem((4,)),
         sem((1,)),
         sem((1,)),
-        sem((n_exp,)),
-        sem((n_exp,)),
+        sem((chips,)),
+        sem((chips,)),
+        sem((2, side)),
+        sem((2, side)),
+        sem((2, side)),
+        sem((2, side)),
+        sem((2, side)),
+        sem((2, side)),
+        sem((heads,)),
         sem((n_ctx,)),
         sem((n_ctx,)),
-        sem((n_ctx,)),
-        sem((n_ctx,)),
-        sem((n_ctx,)),
-        sem((n_ctx,)),
-        sem((n_ctx,)),
-        sem((n_ctx,)),
+        sem((heads,)),
         sem((4, side)),
         sem((4, side)),
         sem((4, side)),
@@ -538,28 +653,13 @@
     out = pl.pallas_call(
         functools.partial(kernel, n_ctx, n_exp, side),
         out_shape=jax.ShapeDtypeStruct((tokens, model), BF16),
-        in_specs=[pl.BlockSpec(memory_space=pltpu.VMEM)] * 14,
+        in_specs=[pl.BlockSpec(memory_space=pltpu.HBM)] * 14,
         out_specs=pl.BlockSpec(memory_space=pltpu.VMEM),
         scratch_shapes=scratch,
         compiler_params=pltpu.CompilerParams(
-            collective_id=0, has_side_effects=True, vmem_limit_bytes=48 * 2**20
+            collective_id=0, has_side_effects=True, vmem_limit_bytes=63 * 2**20
         ),
-    )(
-        qkv[0],
-        taps,
-        lgate[0],
-        beta[0],
-        z[0],
-        gain[None],
-        ow,
-        res[0],
-        post[None],
-        ids[0],
-        rw[0],
-        wg[0],
-        wu[0],
-        wd[0],
-    )
+    )(*operands)
     return out[None]
 
 

time: 196 us -> 168 us (0.86); the launches traced: 193 us -> 168 us
  Pallas kernels: 183 us -> 166 us
  local copies, waits for them, and re-layouts: 10.2 us -> 1.88 us
    pallas_call x1, Pallas kernels: 183 us -> 166 us  [on_device(): pl.pallas_call(functools.partial(kernel, n_ctx, n_exp, side), out_shape=j...]
    unnamed x23 -> x1, local copies, waits for them, and re-layouts: 8.7 us -> 1.88 us
where the time goes in v2:
time: 168 us
  Pallas kernels  166 us (99%)
  local copies, waits for them, and re-layouts  1.88 us (1%)
    pallas_call x1, Pallas kernels, on_device(): pl.pallas_call(functools.partial(kernel, n_ctx, n_exp, side), out_shape=j...  166 us

profile of v2, /device:TPU:1, one launch (start us, length us, event | category | flops | bytes accessed | tf_op | source)
XLA Modules:
  0.0 167.6 jit_solution(14071143465677706565)
XLA Ops:
  0.0 165.7 %shard_map.136 = bf16[128,2048]{1,0:T(8,128)(2,1)} custom-call(bf16[128,3072]{1,0:T(8,128)(2,1)} %bitcast.18, bf16[4,3072]{1,0:T(4,128)(2,1)} %taps_hbm.1, f32[8,128]{1,0:T(8,128)} %bitcast.25, f32[8,128]{1,0:T(8,128)} %bitcast.26, bf16[128,1024]{1,0:T(8,128)(2,1)} %bitcast.20, f32[1,128]{1,0:T(1,128)} %bitcast.27, bf16[32,128]{1,0:T(8,128)(2,1)} %ow_hbm.1, ...), custom_call_target="tpu_custom_call" | custom-call | tf_op jit(solution)/shard_map/pallas_call | solution.py:653
  165.7 1.9 %copy.16 = bf16[1,128,2048]{2,1,0:T(8,128)(2,1)} copy(bf16[1,128,2048]{2,1,0:T(8,128)(2,1)} %bitcast.17) | data formatting | bytes 1048576

commit v3 on v2

--- a/solution.py
+++ b/solution.py
@@ -94,8 +94,17 @@
     arrived,
     answer,
     returned,
+    copy_gate,
+    copy_up,
+    copy_down,
+    row_gate,
+    row_down,
+    col_up,
+    col_down,
     load_s,
     own_s,
+    zx_s,
+    zx_r,
     halo_s,
     halo_r,
     col_s,
@@ -110,10 +119,16 @@
     ab_r,
     st_s,
     st_r,
-    w1_s,
-    w1_r,
-    w2_s,
-    w2_r,
+    g1_s,
+    g1_r,
+    u1_s,
+    u1_r,
+    g2_s,
+    g2_r,
+    u2_s,
+    u2_r,
+    pair_s,
+    pair_r,
     out_s,
     out_r,
     back_s,
@@ -135,20 +150,38 @@
     sibling = exp + 1 - 2 * core
     composer = ctx % 2 == core
 
+    after = chips // 8
+    before = chips // 2 - 1 - after
+    away = 2 * after + 1
+    second, odd = col % 2, row % 2
+    up = 1 - 2 * core
+    my_up = 1 - 2 * odd
+    my_expert = 2 * ((chip + chips - second * away * my_up) % chips) + odd
+    reach = jnp.where(second == 0, before, after)
+    my_block = reach * 4 + odd * 2 + second
+
     barrier = pltpu.get_barrier_semaphore()
 
-    def greet_ctx(d):
+    def greet(to_ctx, to_exp):
         pl.semaphore_signal(
-            barrier, inc=1, device_id={"ctx": (ctx + d) % n_ctx}, device_id_type=MESH
-        )
-
-    def greet_exp(d):
-        pl.semaphore_signal(
-            barrier, inc=1, device_id={"exp": (exp + d) % n_exp}, device_id_type=MESH
-        )
-
-    loop(1, n_ctx, greet_ctx)
-    loop(1, n_exp, greet_exp)
+            barrier, inc=1, device_id={"ctx": to_ctx, "exp": to_exp}, device_id_type=MESH
+        )
+
+    def beside(j):
+        return (row - odd + j // 2) * side + col - second + j % 2
+
+    corner = odd * 2 + second
+    loop(1, n_ctx, lambda d: greet((ctx + d) % n_ctx, exp))
+    loop(0, n_ctx, lambda d: greet((ctx + d) % n_ctx, sibling))
+    loop(1, chips, lambda d: greet(ctx, (exp + 2 * d) % n_exp))
+    for j in range(4):
+
+        @pl.when(j != corner)
+        def _():
+            loop(1, before + 1, lambda d: greet(beside(j), (exp + 2 * d) % n_exp))
+            loop(1, before + 1, lambda d: greet(beside(j), (exp + n_exp - 2 * d) % n_exp))
+
+    greeted = 2 * n_ctx - 1 + chips - 1 + 6 * before
     loads = [
         pltpu.make_async_copy(src, dst, load_s.at[i])
         for i, (src, dst) in enumerate(
@@ -169,26 +202,33 @@
     ]
     for c in loads:
         c.start()
-    owns = [
-        pltpu.make_async_copy(src, dst, own_s.at[i])
-        for i, (src, dst) in enumerate(
-            (
-                (wg_ref, gate_full.at[row, col]),
-                (wu_ref, up_full.at[row, col]),
-                (wd_ref.at[pl.ds(0, wd_ref.shape[0] // 2), :], down_full.at[0, row, col]),
-                (
-                    wd_ref.at[pl.ds(wd_ref.shape[0] // 2, wd_ref.shape[0] // 2), :],
-                    down_full.at[1, row, col],
-                ),
-            )
-        )
+    half_ff = wd_ref.shape[0] // 2
+    wd_first, wd_last = wd_ref.at[pl.ds(0, half_ff), :], wd_ref.at[pl.ds(half_ff, half_ff), :]
+    cd_first = copy_down.at[pl.ds(0, half_ff), :]
+    cd_last = copy_down.at[pl.ds(half_ff, half_ff), :]
+    own_row = [
+        pltpu.make_async_copy(wg_ref, row_gate.at[col], own_s.at[0]),
+        pltpu.make_async_copy(wd_first, row_down.at[col], own_s.at[1]),
     ]
-    for c in owns:
-        c.start()
+    own_col = [
+        pltpu.make_async_copy(wu_ref, col_up.at[0, row], own_s.at[2]),
+        pltpu.make_async_copy(wd_last, col_down.at[0, row], own_s.at[3]),
+    ]
+
+    @pl.when(second == 0)
+    def _():
+        for c in own_row:
+            c.start()
+
+    @pl.when(odd == core)
+    def _():
+        for c in own_col:
+            c.start()
+
     for c in loads[:5]:
         c.wait()
     xs[8:, :] = qkv_ref[...].astype(F32)
-    pl.semaphore_wait(barrier, n_ctx + n_exp - 2)
+    pl.semaphore_wait(barrier, greeted)
 
     halo_copy = copy_to(
         qkv_ref.at[pl.ds(tokens - HALO, HALO), :],
@@ -213,53 +253,93 @@
     def along_y(d):
         return ((row + d) % side) * side + col
 
-    def w1_copies(d):
-        return (
-            copy_to(wg_ref, gate_full.at[row, col], w1_s.at[0, d], w1_r.at[0, d], ctx=along_x(d)),
-            copy_to(wu_ref, up_full.at[row, col], w1_s.at[1, d], w1_r.at[1, d], ctx=along_y(d)),
-            copy_to(
-                wd_ref.at[pl.ds(0, wd_ref.shape[0] // 2), :],
-                down_full.at[0, row, col],
-                w1_s.at[2, d],
-                w1_r.at[2, d],
-                ctx=along_x(d),
-            ),
-            copy_to(
-                wd_ref.at[pl.ds(wd_ref.shape[0] // 2, wd_ref.shape[0] // 2), :],
-                down_full.at[1, row, col],
-                w1_s.at[3, d],
-                w1_r.at[3, d],
-                ctx=along_y(d),
-            ),
-        )
-
-    def w2_copies(d):
-        return (
-            copy_to(
-                gate_full.at[row], gate_full.at[row], w2_s.at[0, d], w2_r.at[0, d], ctx=along_y(d)
-            ),
-            copy_to(
-                up_full.at[:, col], up_full.at[:, col], w2_s.at[1, d], w2_r.at[1, d], ctx=along_x(d)
-            ),
-            copy_to(
-                down_full.at[0, row],
-                down_full.at[0, row],
-                w2_s.at[2, d],
-                w2_r.at[2, d],
-                ctx=along_y(d),
-            ),
-            copy_to(
-                down_full.at[1, :, col],
-                down_full.at[1, :, col],
-                w2_s.at[3, d],
-                w2_r.at[3, d],
-                ctx=along_x(d),
-            ),
-        )
-
-    for d in range(1, side):
-        for c in w1_copies(d):
+    away_exp = 2 * ((chip + chips + away * up) % chips) + core
+    zx_copies = [
+        copy_to(src, dst, zx_s.at[i], zx_r.at[i], exp=away_exp)
+        for i, (src, dst) in enumerate(
+            ((wg_ref, copy_gate), (wu_ref, copy_up), (wd_ref, copy_down))
+        )
+    ]
+
+    def unless(skip, body):
+        def step(i):
+            @pl.when(i != skip)
+            def _():
+                body(i)
+
+        return step
+
+    def g1_copies(kind, to):
+        gate, down = ((wg_ref, wd_first), (copy_gate, cd_first))[kind]
+        there = row * side + to
+        return (
+            copy_to(gate, row_gate.at[col], g1_s.at[0, to], g1_r.at[0, col], ctx=there),
+            copy_to(down, row_down.at[col], g1_s.at[1, to], g1_r.at[1, col], ctx=there),
+        )
+
+    def g1_arrivals(src):
+        there = row * side + src
+        return (
+            copy_to(wg_ref, row_gate.at[src], g1_s.at[0, src], g1_r.at[0, src], ctx=there),
+            copy_to(wd_first, row_down.at[src], g1_s.at[1, src], g1_r.at[1, src], ctx=there),
+        )
+
+    def u1_copies(kind, j):
+        up_src, down = ((wu_ref, wd_last), (copy_up, cd_last))[kind]
+        there = (core + 2 * j) * side + col
+        return (
+            copy_to(
+                up_src, col_up.at[kind, row], u1_s.at[0, kind, j], u1_r.at[0, kind, row], ctx=there
+            ),
+            copy_to(
+                down, col_down.at[kind, row], u1_s.at[1, kind, j], u1_r.at[1, kind, row], ctx=there
+            ),
+        )
+
+    def u1_arrivals(kind, src):
+        there = src * side + col
+        return (
+            copy_to(
+                wu_ref, col_up.at[kind, src], u1_s.at[0, kind, 0], u1_r.at[0, kind, src], ctx=there
+            ),
+            copy_to(
+                wd_last,
+                col_down.at[kind, src],
+                u1_s.at[1, kind, 0],
+                u1_r.at[1, kind, src],
+                ctx=there,
+            ),
+        )
+
+    halves = side // 2
+    row_own = jnp.where(odd == core, row // 2, halves)
+
+    def start_all(copies):
+        for c in copies:
             c.start()
+
+    def wait_sent(copies):
+        for c in copies:
+            c.wait_send()
+
+    def wait_came(copies):
+        for c in copies:
+            c.wait_recv()
+
+    def each_first(kind, act):
+        for j in range(halves):
+            to = 2 * j + kind
+
+            @pl.when(to != col)
+            def _():
+                act(g1_copies(kind, to))
+
+            @pl.when(j != row_own)
+            def _():
+                act(u1_copies(kind, j))
+
+    start_all(zx_copies)
+    each_first(0, start_all)
 
     tri_r = lax.broadcasted_iota(jnp.int32, (tokens, tokens), 0)
     tri_c = lax.broadcasted_iota(jnp.int32, (tokens, tokens), 1)
@@ -384,14 +464,6 @@
     def ab_arrival(src):
         return copy_to(ab_send.at[0], ab_recv.at[src], ab_s.at[0], ab_r.at[src], ctx=src)
 
-    def unless(skip, body):
-        def step(i):
-            @pl.when(i != skip)
-            def _():
-                body(i)
-
-        return step
-
     mine = jnp.where(composer, ctx // 2, n_ctx)
     loop(0, heads, unless(mine, lambda h: ab_copy(h).start()))
 
@@ -445,6 +517,27 @@
         loop(0, n_ctx, unless(ctx, lambda to: st_copy(to).start()))
         st_recv[ctx // 2] = st_send[ctx]
 
+    for c in zx_copies:
+        c.wait_recv()
+    each_first(1, start_all)
+
+    @pl.when(second == 0)
+    def _():
+        for c in own_row:
+            c.wait()
+
+    @pl.when(second == 1)
+    def _():
+        row_gate[col] = copy_gate[...]
+        row_down[col] = copy_down[:half_ff, :]
+
+    @pl.when(odd == core)
+    def _():
+        for c in own_col:
+            c.wait()
+        col_up[1, row] = copy_up[...]
+        col_down[1, row] = copy_down[half_ff:, :]
+
     for d in range(1, side):
         for c, onward in zip(band2_copies(d), core_copies(d)):
             c.wait_send()
@@ -462,15 +555,123 @@
     def _():
         loop(0, n_ctx, unless(ctx, lambda to: st_copy(to).wait_send()))
 
-    for d in range(1, side):
-        for c in w1_copies(d):
-            c.wait_send()
-            c.wait_recv()
-    for c in owns:
-        c.wait()
-    for d in range(1, side):
-        for c in w2_copies(d):
-            c.start()
+    def g2_copies(j):
+        there = (core + 2 * j) * side + col
+        return (
+            copy_to(
+                row_gate, gate_full.at[row], g2_s.at[0, j], g2_r.at[0, row], ctx=there, exp=2 * chip
+            ),
+            copy_to(
+                row_down,
+                down_full.at[0, row],
+                g2_s.at[1, j],
+                g2_r.at[1, row],
+                ctx=there,
+                exp=2 * chip,
+            ),
+        )
+
+    def g2_arrivals(src):
+        there = src * side + col
+        return (
+            copy_to(
+                row_gate,
+                gate_full.at[src],
+                g2_s.at[0, 0],
+                g2_r.at[0, src],
+                ctx=there,
+                exp=2 * chip + odd,
+            ),
+            copy_to(
+                row_down,
+                down_full.at[0, src],
+                g2_s.at[1, 0],
+                g2_r.at[1, src],
+                ctx=there,
+                exp=2 * chip + odd,
+            ),
+        )
+
+    def u2_copies(kind, j):
+        there = row * side + 2 * j + kind
+        return (
+            copy_to(
+                col_up.at[kind],
+                up_full.at[:, col],
+                u2_s.at[0, kind, j],
+                u2_r.at[0, col],
+                ctx=there,
+                exp=2 * chip + 1,
+            ),
+            copy_to(
+                col_down.at[kind],
+                down_full.at[1, :, col],
+                u2_s.at[1, kind, j],
+                u2_r.at[1, col],
+                ctx=there,
+                exp=2 * chip + 1,
+            ),
+        )
+
+    def u2_arrivals(src):
+        there = row * side + src
+        return (
+            copy_to(
+                col_up.at[0],
+                up_full.at[:, src],
+                u2_s.at[0, 0, 0],
+                u2_r.at[0, src],
+                ctx=there,
+                exp=2 * chip + odd,
+            ),
+            copy_to(
+                col_down.at[0],
+                down_full.at[1, :, src],
+                u2_s.at[1, 0, 0],
+                u2_r.at[1, src],
+                ctx=there,
+                exp=2 * chip + odd,
+            ),
+        )
+
+    g2_own = jnp.where(jnp.logical_and(core == 0, odd == 0), row // 2, halves)
+    u2_own = jnp.where(jnp.logical_and(core == 1, odd == 1), col, side)
+
+    def each_second(act):
+        for j in range(halves):
+
+            @pl.when(j != g2_own)
+            def _():
+                act(g2_copies(j))
+
+        @pl.when(odd == core)
+        def _():
+            for kind in range(2):
+                for j in range(halves):
+
+                    @pl.when(2 * j + kind != u2_own)
+                    def _():
+                        act(u2_copies(kind, j))
+
+    loop(0, side, unless(col, lambda src: wait_came(g1_arrivals(src))))
+
+    @pl.when(odd == core)
+    def _():
+        for kind in range(2):
+            loop(0, side, unless(row, lambda src: wait_came(u1_arrivals(kind, src))))
+
+    each_second(start_all)
+
+    @pl.when(g2_own < halves)
+    def _():
+        gate_full[row] = row_gate[...]
+        down_full[0, row] = row_down[...]
+
+    @pl.when(u2_own < side)
+    def _():
+        for r in range(side):
+            up_full[r, col] = col_up[second, r]
+            down_full[1, r, col] = col_down[second, r]
 
     for c in loads[5:]:
         c.wait()
@@ -509,24 +710,102 @@
     sent = dot(pick_low, routed_in[:, :halfm], TN) + dot(pick_high, routed_in[:, halfm:], TN)
     outbound[...] = sent.astype(BF16).reshape(outbound.shape)
 
-    def out_copy(d):
-        to = (exp + d) % n_exp
-        return copy_to(outbound.at[to], arrived.at[exp], out_s.at[d], out_r.at[d], exp=to)
-
-    loop(1, n_exp, lambda d: out_copy(d).start())
-    arrived[exp] = outbound[exp]
-
-    for d in range(1, side):
-        for c in w2_copies(d):
-            c.wait_send()
-            c.wait_recv()
-
-    def out_wait(d):
-        c = out_copy(d)
-        c.wait_send()
-        c.wait_recv()
-
-    loop(1, n_exp, out_wait)
+    def out_copy(k, c):
+        rise = 1 - 2 * c
+        place = (-k * rise) % chips
+        spread = (place + before) % chips
+        if spread < chips // 2:
+            kind, shift = 0, k % chips
+        else:
+            kind, shift, spread = 1, (k + away * rise) % chips, spread - chips // 2
+        to_ctx = (row - odd + c) * side + col - second + kind
+        to_exp = (exp + 2 * shift) % n_exp
+        block = spread * 4 + odd * 2 + second
+        what = copy_to(
+            outbound.at[(2 * chip + 2 * k) % n_exp + c],
+            arrived.at[block],
+            out_s.at[2 * k + c],
+            out_r.at[block],
+            ctx=to_ctx,
+            exp=to_exp,
+        )
+        if shift:
+            return what, None
+        return what, jnp.logical_and(odd == c, second == kind)
+
+    def each_out(act):
+        for k in range(chips):
+            for c in range(2):
+                what, here = out_copy(k, c)
+                if here is None:
+                    act([what])
+                else:
+
+                    @pl.when(jnp.logical_not(here))
+                    def _():
+                        act([what])
+
+    each_out(start_all)
+    arrived[my_block] = outbound[my_expert]
+
+    def pair_copies(i, which):
+        parts = (
+            (gate_full.at[i], down_full.at[0, i]),
+            (up_full.at[:, i], down_full.at[1, :, i]),
+        )[which]
+        return [
+            copy_to(
+                part, part, pair_s.at[2 * which + n, i], pair_r.at[2 * which + n, i], exp=sibling
+            )
+            for n, part in enumerate(parts)
+        ]
+
+    @pl.when(core == 0)
+    def _():
+        def onward(src):
+            @pl.when(jnp.logical_or(src != row, odd == 1))
+            def _():
+                wait_came(g2_arrivals(src))
+
+            start_all(pair_copies(src, 0))
+
+        loop(0, side, onward)
+
+    @pl.when(core == 1)
+    def _():
+        def onward(src):
+            @pl.when(jnp.logical_or(src != col, odd == 0))
+            def _():
+                wait_came(u2_arrivals(src))
+
+            start_all(pair_copies(src, 1))
+
+        loop(0, side, onward)
+
+    wait_sent(zx_copies)
+    each_first(0, wait_sent)
+    each_first(1, wait_sent)
+    each_second(wait_sent)
+
+    @pl.when(core == 0)
+    def _():
+        for i in range(side):
+            wait_sent(pair_copies(i, 0))
+            wait_came(pair_copies(i, 1))
+
+    @pl.when(core == 1)
+    def _():
+        for i in range(side):
+            wait_sent(pair_copies(i, 1))
+            wait_came(pair_copies(i, 0))
+
+    def out_arrival(block):
+        return copy_to(
+            outbound.at[0], arrived.at[block], out_s.at[0], out_r.at[block], exp=sibling
+        )
+
+    loop(0, n_exp, unless(my_block, lambda block: out_arrival(block).wait_recv()))
+    each_out(wait_sent)
 
     ff = wg_ref.shape[1]
     came = arrived[...].astype(F32)
@@ -550,19 +829,26 @@
             parts.append(dot(activated, down).reshape(n_exp, cap, lanes))
         answer[:, :, j * lanes : (j + 1) * lanes] = jnp.concatenate(parts, axis=1).astype(BF16)
 
-    def back_copy(d):
-        to = (exp + d) % n_exp
-        return copy_to(answer.at[to], returned.at[exp], back_s.at[d], back_r.at[d], exp=to)
-
-    loop(1, n_exp, lambda d: back_copy(d).start())
-    returned[exp] = answer[exp]
-
-    def back_wait(d):
-        c = back_copy(d)
-        c.wait_send()
-        c.wait_recv()
-
-    loop(1, n_exp, back_wait)
+    def back_copy(block):
+        far = (block // 4 + chips - reach) * my_up + 2 * chips
+        return copy_to(
+            answer.at[block],
+            returned.at[my_expert],
+            back_s.at[block],
+            back_r.at[my_expert],
+            ctx=beside(block % 4),
+            exp=2 * ((chip + far) % chips) + core,
+        )
+
+    def back_arrival(expert):
+        return copy_to(
+            answer.at[0], returned.at[expert], back_s.at[0], back_r.at[expert], exp=sibling
+        )
+
+    loop(0, n_exp, unless(my_block, lambda block: back_copy(block).start()))
+    returned[my_expert] = answer[my_block]
+    loop(0, n_exp, unless(my_expert, lambda expert: back_arrival(expert).wait_recv()))
+    loop(0, n_exp, unless(my_block, lambda block: back_copy(block).wait_send()))
 
     back = returned[...].reshape(2 * cap * n_exp, halfm)
     weight = column(rw_ref[...])
@@ -625,8 +911,17 @@
         pltpu.VMEM(slots, BF16),
         pltpu.VMEM(slots, BF16),
         pltpu.VMEM(slots, BF16),
+        pltpu.VMEM((model // n_ctx, ff), BF16),
+        pltpu.VMEM((model // n_ctx, ff), BF16),
+        pltpu.VMEM((ff, lanes), BF16),
+        pltpu.VMEM((side, model // n_ctx, ff), BF16),
+        pltpu.VMEM((side, ff // 2, lanes), BF16),
+        pltpu.VMEM((2, side, model // n_ctx, ff), BF16),
+        pltpu.VMEM((2, side, ff // 2, lanes), BF16),
         sem((11,)),
         sem((4,)),
+        sem((3,)),
+        sem((3,)),
         sem((1,)),
         sem((1,)),
         sem((chips,)),
@@ -641,8 +936,14 @@
         sem((n_ctx,)),
         sem((n_ctx,)),
         sem((heads,)),
-        sem((4, side)),
-        sem((4, side)),
+        sem((2, side)),
+        sem((2, side)),
+        sem((2, 2, side)),
+        sem((2, 2, side)),
+        sem((2, side)),
+        sem((2, side)),
+        sem((2, 2, side)),
+        sem((2, side)),
         sem((4, side)),
         sem((4, side)),
         sem((n_exp,)),

time: 168 us -> 149 us (0.89)
  the two profiles are of different devices: /device:TPU:1 before, /device:TPU:40 now
where the time goes in v3:
time: 149 us; the launch traced here: 148 us
  Pallas kernels  146 us (98%)
  local copies, waits for them, and re-layouts  1.88 us (1%)
    pallas_call x1, Pallas kernels, on_device(): pl.pallas_call(functools.partial(kernel, n_ctx, n_exp, side), out_shape=j...  146 us

profile of v3, /device:TPU:40, one launch (start us, length us, event | category | flops | bytes accessed | tf_op | source)
XLA Modules:
  0.0 148.3 jit_solution(106114447571728478)
XLA Ops:
  0.0 146.5 %shard_map.136 = bf16[128,2048]{1,0:T(8,128)(2,1)} custom-call(bf16[128,3072]{1,0:T(8,128)(2,1)} %bitcast.18, bf16[4,3072]{1,0:T(4,128)(2,1)} %taps_hbm.1, f32[8,128]{1,0:T(8,128)} %bitcast.25, f32[8,128]{1,0:T(8,128)} %bitcast.26, bf16[128,1024]{1,0:T(8,128)(2,1)} %bitcast.20, f32[1,128]{1,0:T(1,128)} %bitcast.27, bf16[32,128]{1,0:T(8,128)(2,1)} %ow_hbm.1, ...), custom_call_target="tpu_custom_call" | custom-call | tf_op jit(solution)/shard_map/pallas_call | solution.py:954
  146.5 1.9 %copy.16 = bf16[1,128,2048]{2,1,0:T(8,128)(2,1)} copy(bf16[1,128,2048]{2,1,0:T(8,128)(2,1)} %bitcast.17) | data formatting | bytes 1048576

commit v4 on v3

--- a/solution.py
+++ b/solution.py
@@ -154,8 +154,9 @@
     before = chips // 2 - 1 - after
     away = 2 * after + 1
     second, odd = col % 2, row % 2
-    up = 1 - 2 * core
-    my_up = 1 - 2 * odd
+    up = 1 - 2 * ((chip + core) % 2)
+    turn = 1 - 2 * (chip % 2)
+    my_up = turn * (1 - 2 * odd) * (1 - 2 * second)
     my_expert = 2 * ((chip + chips - second * away * my_up) % chips) + odd
     reach = jnp.where(second == 0, before, after)
     my_block = reach * 4 + odd * 2 + second
@@ -387,6 +388,44 @@
         kk = dot(k, k, NT)
         lowers.append(jnp.where(strict, strength[h] * decay * kk, 0.0))
 
+    def col_wait(d):
+        c = col_copy(d)
+        c.wait_send()
+        c.wait_recv()
+
+    loop(1, chips, col_wait)
+    fore, rear = pl.ds(0, chips // 2), pl.ds(chips // 2, chips // 2)
+
+    def band1_copies(d):
+        return (
+            copy_to(
+                colblk.at[fore],
+                wbuf.at[row, col, fore, core],
+                band1_s.at[0, d],
+                band1_r.at[0, d],
+                ctx=along_x(d),
+            ),
+            copy_to(
+                colblk.at[rear],
+                wbuf.at[row, col, rear, core],
+                band1_s.at[1, d],
+                band1_r.at[1, d],
+                ctx=along_y(d),
+            ),
+        )
+
+    def band2_copies(d):
+        ahead, behind = wbuf.at[row, :, fore, core], wbuf.at[:, col, rear, core]
+        return (
+            copy_to(ahead, ahead, band2_s.at[0, d], band2_r.at[0, d], ctx=along_y(d)),
+            copy_to(behind, behind, band2_s.at[1, d], band2_r.at[1, d], ctx=along_x(d)),
+        )
+
+    for d in range(1, side):
+        for c in band1_copies(d):
+            c.start()
+    wbuf[row, col, :, core] = colblk[...]
+
     def same(size):
         return tri_r // size == tri_c // size
 
@@ -404,44 +443,14 @@
         inv = [x - dot(x, m) for x, m in zip(inv, mid)]
         size *= 2
 
-    def col_wait(d):
-        c = col_copy(d)
-        c.wait_send()
-        c.wait_recv()
-
-    loop(1, chips, col_wait)
-    fore, rear = pl.ds(0, chips // 2), pl.ds(chips // 2, chips // 2)
-
-    def band1_copies(d):
-        return (
-            copy_to(
-                colblk.at[fore],
-                wbuf.at[row, col, fore, core],
-                band1_s.at[0, d],
-                band1_r.at[0, d],
-                ctx=along_x(d),
-            ),
-            copy_to(
-                colblk.at[rear],
-                wbuf.at[row, col, rear, core],
-                band1_s.at[1, d],
-                band1_r.at[1, d],
-                ctx=along_y(d),
-            ),
-        )
-
-    def band2_copies(d):
-        ahead, behind = wbuf.at[row, :, fore, core], wbuf.at[:, col, rear, core]
-        return (
-            copy_to(ahead, ahead, band2_s.at[0, d], band2_r.at[0, d], ctx=along_y(d)),
-            copy_to(behind, behind, band2_s.at[1, d], band2_r.at[1, d], ctx=along_x(d)),
-        )
-
-    for d in range(1, side):
-        for c in band1_copies(d):
-            c.start()
-    wbuf[row, col, :, core] = colblk[...]
-
+    def ab_copy(h):
+        to = 2 * h + core
+        return copy_to(ab_send.at[h], ab_recv.at[ctx], ab_s.at[h], ab_r.at[ctx], ctx=to)
+
+    def ab_arrival(src):
+        return copy_to(ab_send.at[0], ab_recv.at[src], ab_s.at[0], ab_r.at[src], ctx=src)
+
+    mine = jnp.where(composer, ctx // 2, n_ctx)
     for h in range(heads):
         b = strength[h]
         gc = growth_col[h]
@@ -457,19 +466,33 @@
         ab_send[h, :HD, :] = at
         ab_send[h, HD:, :] = bt
 
-    def ab_copy(h):
-        to = 2 * h + core
-        return copy_to(ab_send.at[h], ab_recv.at[ctx], ab_s.at[h], ab_r.at[ctx], ctx=to)
-
-    def ab_arrival(src):
-        return copy_to(ab_send.at[0], ab_recv.at[src], ab_s.at[0], ab_r.at[src], ctx=src)
-
-    mine = jnp.where(composer, ctx // 2, n_ctx)
-    loop(0, heads, unless(mine, lambda h: ab_copy(h).start()))
+        @pl.when(h != mine)
+        def _():
+            ab_copy(h).start()
 
     @pl.when(composer)
     def _():
         ab_recv[ctx] = ab_send[ctx // 2]
+
+
+    for d in range(1, side):
+        for c in band1_copies(d):
+            c.wait_send()
+            c.wait_recv()
+    for d in range(1, side):
+        for c in band2_copies(d):
+            c.start()
+
+    def core_copies(d):
+        r, q = (row + side - d) % side, (col + side - d) % side
+        ahead, behind = wbuf.at[r, :, fore, core], wbuf.at[:, q, rear, core]
+        return (
+            copy_to(ahead, ahead, core_s.at[0, d], core_r.at[0, d], exp=sibling),
+            copy_to(behind, behind, core_s.at[1, d], core_r.at[1, d], exp=sibling),
+        )
+
+    for c in core_copies(0):
+        c.start()
 
     for h in range(heads):
         gc = growth_col[h]
@@ -479,25 +502,6 @@
         qmap[h] = (jnp.exp(gc) * q - both[:, :HD]).astype(BF16)
         lout[h] = both[:, HD:]
 
-    for d in range(1, side):
-        for c in band1_copies(d):
-            c.wait_send()
-            c.wait_recv()
-    for d in range(1, side):
-        for c in band2_copies(d):
-            c.start()
-
-    def core_copies(d):
-        r, q = (row + side - d) % side, (col + side - d) % side
-        ahead, behind = wbuf.at[r, :, fore, core], wbuf.at[:, q, rear, core]
-        return (
-            copy_to(ahead, ahead, core_s.at[0, d], core_r.at[0, d], exp=sibling),
-            copy_to(behind, behind, core_s.at[1, d], core_r.at[1, d], exp=sibling),
-        )
-
-    for c in core_copies(0):
-        c.start()
-
     def st_copy(to):
         return copy_to(
             st_send.at[to], st_recv.at[ctx // 2], st_s.at[to], st_r.at[ctx // 2], ctx=to
@@ -510,11 +514,15 @@
         for c in range(n_ctx):
             high = state.astype(BF16)
             st_send[c] = high
+
+            @pl.when(ctx != c)
+            def _():
+                st_copy(c).start()
+
             if c < n_ctx - 1:
                 low = (state - high.astype(F32)).astype(BF16)
                 parts = dot(jnp.concatenate([high, low], axis=0), ab_recv[c, :HD, :])
                 state = parts[:HD] + parts[HD:] + ab_recv[c, HD:, :].astype(F32)
-        loop(0, n_ctx, unless(ctx, lambda to: st_copy(to).start()))
         st_recv[ctx // 2] = st_send[ctx]
 
     for c in zx_copies:
@@ -711,7 +719,7 @@
     outbound[...] = sent.astype(BF16).reshape(outbound.shape)
 
     def out_copy(k, c):
-        rise = 1 - 2 * c
+        rise = 1 - 2 * ((k + c) % 2)
         place = (-k * rise) % chips
         spread = (place + before) % chips
         if spread < chips // 2:
@@ -719,10 +727,10 @@
         else:
             kind, shift, spread = 1, (k + away * rise) % chips, spread - chips // 2
         to_ctx = (row - odd + c) * side + col - second + kind
-        to_exp = (exp + 2 * shift) % n_exp
+        to_exp = (exp + 2 * turn * shift + 2 * n_exp) % n_exp
         block = spread * 4 + odd * 2 + second
         what = copy_to(
-            outbound.at[(2 * chip + 2 * k) % n_exp + c],
+            outbound.at[(2 * chip + 2 * turn * k + 2 * n_exp) % n_exp + c],
             arrived.at[block],
             out_s.at[2 * k + c],
             out_r.at[block],

time: 149 us -> 137 us (0.919)
  the two profiles are of different devices: /device:TPU:40 before, /device:TPU:105 now
where the time goes in v4:
time: 137 us
  Pallas kernels  135 us (99%)
  local copies, waits for them, and re-layouts  1.88 us (1%)
    pallas_call x1, Pallas kernels, on_device(): pl.pallas_call(functools.partial(kernel, n_ctx, n_exp, side), out_shape=j...  135 us

profile of v4, /device:TPU:105, one launch (start us, length us, event | category | flops | bytes accessed | tf_op | source)
XLA Modules:
  0.0 137.3 jit_solution(7556745791232620684)
XLA Ops:
  0.0 135.4 %shard_map.136 = bf16[128,2048]{1,0:T(8,128)(2,1)} custom-call(bf16[128,3072]{1,0:T(8,128)(2,1)} %bitcast.18, bf16[4,3072]{1,0:T(4,128)(2,1)} %taps_hbm.1, f32[8,128]{1,0:T(8,128)} %bitcast.25, f32[8,128]{1,0:T(8,128)} %bitcast.26, bf16[128,1024]{1,0:T(8,128)(2,1)} %bitcast.20, f32[1,128]{1,0:T(1,128)} %bitcast.27, bf16[32,128]{1,0:T(8,128)(2,1)} %ow_hbm.1, ...), custom_call_target="tpu_custom_call" | custom-call | tf_op jit(solution)/shard_map/pallas_call | solution.py:962
  135.4 1.9 %copy.16 = bf16[1,128,2048]{2,1,0:T(8,128)(2,1)} copy(bf16[1,128,2048]{2,1,0:T(8,128)(2,1)} %bitcast.17) | data formatting | bytes 1048576

commit v5 on v4

--- a/solution.py
+++ b/solution.py
@@ -339,7 +339,6 @@
             def _():
                 act(u1_copies(kind, j))
 
-    start_all(zx_copies)
     each_first(0, start_all)
 
     tri_r = lax.broadcasted_iota(jnp.int32, (tokens, tokens), 0)
@@ -362,7 +361,7 @@
     growth_col = [column(g) for g in growth]
     last = [g[:, tokens - 1 :] for g in growth]
     strength = [column(beta_ref[h : h + 1, :]) for h in range(heads)]
-    halo_copy.wait()
+    halo_copy.wait_recv()
     xs[:8, :] = jnp.where(ctx > 0, halo[...].astype(F32)[HALO - 8 :, :], 0.0)
     taps = taps_ref[...].astype(F32)
 
@@ -388,12 +387,8 @@
         kk = dot(k, k, NT)
         lowers.append(jnp.where(strict, strength[h] * decay * kk, 0.0))
 
-    def col_wait(d):
-        c = col_copy(d)
-        c.wait_send()
-        c.wait_recv()
-
-    loop(1, chips, col_wait)
+    loop(1, chips, lambda d: col_copy(d).wait_recv())
+    start_all(zx_copies)
     fore, rear = pl.ds(0, chips // 2), pl.ds(chips // 2, chips // 2)
 
     def band1_copies(d):
@@ -476,9 +471,7 @@
 
 
     for d in range(1, side):
-        for c in band1_copies(d):
-            c.wait_send()
-            c.wait_recv()
+        wait_came(band1_copies(d))
     for d in range(1, side):
         for c in band2_copies(d):
             c.start()
@@ -525,30 +518,8 @@
                 state = parts[:HD] + parts[HD:] + ab_recv[c, HD:, :].astype(F32)
         st_recv[ctx // 2] = st_send[ctx]
 
-    for c in zx_copies:
-        c.wait_recv()
-    each_first(1, start_all)
-
-    @pl.when(second == 0)
-    def _():
-        for c in own_row:
-            c.wait()
-
-    @pl.when(second == 1)
-    def _():
-        row_gate[col] = copy_gate[...]
-        row_down[col] = copy_down[:half_ff, :]
-
-    @pl.when(odd == core)
-    def _():
-        for c in own_col:
-            c.wait()
-        col_up[1, row] = copy_up[...]
-        col_down[1, row] = copy_down[half_ff:, :]
-
     for d in range(1, side):
         for c, onward in zip(band2_copies(d), core_copies(d)):
-            c.wait_send()
             c.wait_recv()
             onward.start()
 
@@ -557,130 +528,6 @@
         return copy_to(st_send.at[0], st_recv.at[h], st_s.at[0], st_r.at[h], ctx=src)
 
     loop(0, heads, unless(mine, lambda h: st_arrival(h).wait_recv()))
-    loop(0, heads, unless(mine, lambda h: ab_copy(h).wait_send()))
-
-    @pl.when(composer)
-    def _():
-        loop(0, n_ctx, unless(ctx, lambda to: st_copy(to).wait_send()))
-
-    def g2_copies(j):
-        there = (core + 2 * j) * side + col
-        return (
-            copy_to(
-                row_gate, gate_full.at[row], g2_s.at[0, j], g2_r.at[0, row], ctx=there, exp=2 * chip
-            ),
-            copy_to(
-                row_down,
-                down_full.at[0, row],
-                g2_s.at[1, j],
-                g2_r.at[1, row],
-                ctx=there,
-                exp=2 * chip,
-            ),
-        )
-
-    def g2_arrivals(src):
-        there = src * side + col
-        return (
-            copy_to(
-                row_gate,
-                gate_full.at[src],
-                g2_s.at[0, 0],
-                g2_r.at[0, src],
-                ctx=there,
-                exp=2 * chip + odd,
-            ),
-            copy_to(
-                row_down,
-                down_full.at[0, src],
-                g2_s.at[1, 0],
-                g2_r.at[1, src],
-                ctx=there,
-                exp=2 * chip + odd,
-            ),
-        )
-
-    def u2_copies(kind, j):
-        there = row * side + 2 * j + kind
-        return (
-            copy_to(
-                col_up.at[kind],
-                up_full.at[:, col],
-                u2_s.at[0, kind, j],
-                u2_r.at[0, col],
-                ctx=there,
-                exp=2 * chip + 1,
-            ),
-            copy_to(
-                col_down.at[kind],
-                down_full.at[1, :, col],
-                u2_s.at[1, kind, j],
-                u2_r.at[1, col],
-                ctx=there,
-                exp=2 * chip + 1,
-            ),
-        )
-
-    def u2_arrivals(src):
-        there = row * side + src
-        return (
-            copy_to(
-                col_up.at[0],
-                up_full.at[:, src],
-                u2_s.at[0, 0, 0],
-                u2_r.at[0, src],
-                ctx=there,
-                exp=2 * chip + odd,
-            ),
-            copy_to(
-                col_down.at[0],
-                down_full.at[1, :, src],
-                u2_s.at[1, 0, 0],
-                u2_r.at[1, src],
-                ctx=there,
-                exp=2 * chip + odd,
-            ),
-        )
-
-    g2_own = jnp.where(jnp.logical_and(core == 0, odd == 0), row // 2, halves)
-    u2_own = jnp.where(jnp.logical_and(core == 1, odd == 1), col, side)
-
-    def each_second(act):
-        for j in range(halves):
-
-            @pl.when(j != g2_own)
-            def _():
-                act(g2_copies(j))
-
-        @pl.when(odd == core)
-        def _():
-            for kind in range(2):
-                for j in range(halves):
-
-                    @pl.when(2 * j + kind != u2_own)
-                    def _():
-                        act(u2_copies(kind, j))
-
-    loop(0, side, unless(col, lambda src: wait_came(g1_arrivals(src))))
-
-    @pl.when(odd == core)
-    def _():
-        for kind in range(2):
-            loop(0, side, unless(row, lambda src: wait_came(u1_arrivals(kind, src))))
-
-    each_second(start_all)
-
-    @pl.when(g2_own < halves)
-    def _():
-        gate_full[row] = row_gate[...]
-        down_full[0, row] = row_down[...]
-
-    @pl.when(u2_own < side)
-    def _():
-        for r in range(side):
-            up_full[r, col] = col_up[second, r]
-            down_full[1, r, col] = col_down[second, r]
-
     for c in loads[5:]:
         c.wait()
     gain = gain_ref[...]
@@ -690,10 +537,29 @@
         z = z_ref[:, h * HD : (h + 1) * HD].astype(F32)
         normed[:, h * HD : (h + 1) * HD] = (read * scale * gain * silu(z)).astype(BF16)
 
+    for c in zx_copies:
+        c.wait_recv()
+    each_first(1, start_all)
+
+    @pl.when(second == 0)
+    def _():
+        for c in own_row:
+            c.wait()
+
+    @pl.when(second == 1)
+    def _():
+        row_gate[col] = copy_gate[...]
+        row_down[col] = copy_down[:half_ff, :]
+
+    @pl.when(odd == core)
+    def _():
+        for c in own_col:
+            c.wait()
+        col_up[1, row] = copy_up[...]
+        col_down[1, row] = copy_down[half_ff:, :]
+
     for d in range(side):
-        for c in core_copies(d):
-            c.wait_send()
-            c.wait_recv()
+        wait_came(core_copies(d))
 
     squares = jnp.zeros((tokens, 1), F32)
     act = normed[...]
@@ -756,6 +622,124 @@
     each_out(start_all)
     arrived[my_block] = outbound[my_expert]
 
+    def g2_copies(j):
+        there = (core + 2 * j) * side + col
+        return (
+            copy_to(
+                row_gate, gate_full.at[row], g2_s.at[0, j], g2_r.at[0, row], ctx=there, exp=2 * chip
+            ),
+            copy_to(
+                row_down,
+                down_full.at[0, row],
+                g2_s.at[1, j],
+                g2_r.at[1, row],
+                ctx=there,
+                exp=2 * chip,
+            ),
+        )
+
+    def g2_arrivals(src):
+        there = src * side + col
+        return (
+            copy_to(
+                row_gate,
+                gate_full.at[src],
+                g2_s.at[0, 0],
+                g2_r.at[0, src],
+                ctx=there,
+                exp=2 * chip + odd,
+            ),
+            copy_to(
+                row_down,
+                down_full.at[0, src],
+                g2_s.at[1, 0],
+                g2_r.at[1, src],
+                ctx=there,
+                exp=2 * chip + odd,
+            ),
+        )
+
+    def u2_copies(kind, j):
+        there = row * side + 2 * j + kind
+        return (
+            copy_to(
+                col_up.at[kind],
+                up_full.at[:, col],
+                u2_s.at[0, kind, j],
+                u2_r.at[0, col],
+                ctx=there,
+                exp=2 * chip + 1,
+            ),
+            copy_to(
+                col_down.at[kind],
+                down_full.at[1, :, col],
+                u2_s.at[1, kind, j],
+                u2_r.at[1, col],
+                ctx=there,
+                exp=2 * chip + 1,
+            ),
+        )
+
+    def u2_arrivals(src):
+        there = row * side + src
+        return (
+            copy_to(
+                col_up.at[0],
+                up_full.at[:, src],
+                u2_s.at[0, 0, 0],
+                u2_r.at[0, src],
+                ctx=there,
+                exp=2 * chip + odd,
+            ),
+            copy_to(
+                col_down.at[0],
+                down_full.at[1, :, src],
+                u2_s.at[1, 0, 0],
+                u2_r.at[1, src],
+                ctx=there,
+                exp=2 * chip + odd,
+            ),
+        )
+
+    g2_own = jnp.where(jnp.logical_and(core == 0, odd == 0), row // 2, halves)
+    u2_own = jnp.where(jnp.logical_and(core == 1, odd == 1), col, side)
+
+    def each_second(act):
+        for j in range(halves):
+
+            @pl.when(j != g2_own)
+            def _():
+                act(g2_copies(j))
+
+        @pl.when(odd == core)
+        def _():
+            for kind in range(2):
+                for j in range(halves):
+
+                    @pl.when(2 * j + kind != u2_own)
+                    def _():
+                        act(u2_copies(kind, j))
+
+    loop(0, side, unless(col, lambda src: wait_came(g1_arrivals(src))))
+
+    @pl.when(odd == core)
+    def _():
+        for kind in range(2):
+            loop(0, side, unless(row, lambda src: wait_came(u1_arrivals(kind, src))))
+
+    each_second(start_all)
+
+    @pl.when(g2_own < halves)
+    def _():
+        gate_full[row] = row_gate[...]
+        down_full[0, row] = row_down[...]
+
+    @pl.when(u2_own < side)
+    def _():
+        for r in range(side):
+            up_full[r, col] = col_up[second, r]
+            down_full[1, r, col] = col_down[second, r]
+
     def pair_copies(i, which):
         parts = (
             (gate_full.at[i], down_full.at[0, i]),
@@ -790,21 +774,14 @@
 
         loop(0, side, onward)
 
-    wait_sent(zx_copies)
-    each_first(0, wait_sent)
-    each_first(1, wait_sent)
-    each_second(wait_sent)
-
     @pl.when(core == 0)
     def _():
         for i in range(side):
-            wait_sent(pair_copies(i, 0))
             wait_came(pair_copies(i, 1))
 
     @pl.when(core == 1)
     def _():
         for i in range(side):
-            wait_sent(pair_copies(i, 1))
             wait_came(pair_copies(i, 0))
 
     def out_arrival(block):
@@ -813,8 +790,6 @@
         )
 
     loop(0, n_exp, unless(my_block, lambda block: out_arrival(block).wait_recv()))
-    each_out(wait_sent)
-
     ff = wg_ref.shape[1]
     came = arrived[...].astype(F32)
     rows_in = jnp.concatenate(
@@ -855,8 +830,38 @@
 
     loop(0, n_exp, unless(my_block, lambda block: back_copy(block).start()))
     returned[my_expert] = answer[my_block]
+
+    halo_copy.wait_send()
+    loop(1, chips, lambda d: col_copy(d).wait_send())
+    for d in range(1, side):
+        wait_sent(band1_copies(d))
+        wait_sent(band2_copies(d))
+    for d in range(side):
+        wait_sent(core_copies(d))
+    loop(0, heads, unless(mine, lambda h: ab_copy(h).wait_send()))
+
+    @pl.when(composer)
+    def _():
+        loop(0, n_ctx, unless(ctx, lambda to: st_copy(to).wait_send()))
+
+    wait_sent(zx_copies)
+    each_first(0, wait_sent)
+    each_first(1, wait_sent)
+    each_second(wait_sent)
+
+    @pl.when(core == 0)
+    def _():
+        for i in range(side):
+            wait_sent(pair_copies(i, 0))
+
+    @pl.when(core == 1)
+    def _():
+        for i in range(side):
+            wait_sent(pair_copies(i, 1))
+
+    each_out(wait_sent)
+    loop(0, n_exp, unless(my_block, lambda block: back_copy(block).wait_send()))
     loop(0, n_exp, unless(my_expert, lambda expert: back_arrival(expert).wait_recv()))
-    loop(0, n_exp, unless(my_block, lambda block: back_copy(block).wait_send()))
 
     back = returned[...].reshape(2 * cap * n_exp, halfm)
     weight = column(rw_ref[...])

time: 137 us -> 134 us (0.978)
  the two profiles are of different devices: /device:TPU:105 before, /device:TPU:121 now
where the time goes in v5:
time: 134 us
  Pallas kernels  132 us (99%)
  local copies, waits for them, and re-layouts  1.88 us (1%)
    pallas_call x1, Pallas kernels, on_device(): pl.pallas_call(functools.partial(kernel, n_ctx, n_exp, side), out_shape=j...  132 us

profile of v5, /device:TPU:121, one launch (start us, length us, event | category | flops | bytes accessed | tf_op | source)
XLA Modules:
  0.0 134.2 jit_solution(151892551858092174)
XLA Ops:
  0.0 132.3 %shard_map.136 = bf16[128,2048]{1,0:T(8,128)(2,1)} custom-call(bf16[128,3072]{1,0:T(8,128)(2,1)} %bitcast.18, bf16[4,3072]{1,0:T(4,128)(2,1)} %taps_hbm.1, f32[8,128]{1,0:T(8,128)} %bitcast.25, f32[8,128]{1,0:T(8,128)} %bitcast.26, bf16[128,1024]{1,0:T(8,128)(2,1)} %bitcast.20, f32[1,128]{1,0:T(1,128)} %bitcast.27, bf16[32,128]{1,0:T(8,128)(2,1)} %ow_hbm.1, ...), custom_call_target="tpu_custom_call" | custom-call | tf_op jit(solution)/shard_map/pallas_call | solution.py:967
  132.3 1.9 %copy.16 = bf16[1,128,2048]{2,1,0:T(8,128)(2,1)} copy(bf16[1,128,2048]{2,1,0:T(8,128)(2,1)} %bitcast.17) | data formatting | bytes 1048576
